TPU v7x, 512 devices: a whole 4x4x16 slice. The times are simulated.
512 devices in a mesh: gx: 32 (over x, y, core), gy: 16 (over z).
Axes of the slice: x: 4, y: 4, z: 16, core: 2. Of those that a mesh axis runs over, the one named last changes fastest.
Arguments:
- positions: float32 [3, 32, 16, 128], P(None, 'gx', 'gy'), may hold values from 0 to 384, as said below
- neighbours: int32 [32, 32, 16, 128], P(None, 'gx', 'gy'), may hold values from 0 to 1151, as said below
- live_count: int32 [32, 16], P('gx', 'gy'), may hold values from 16 to 128, as said below
- stencil_base: int32 [3, 32, 16, 128], P(None, 'gx', 'gy'), may hold values from -1 to 383, as said below
- spline_weight: float32 [3, 4, 32, 16, 128], P(None, None, 'gx', 'gy'), may hold values from 0 to 1, as said below
- spline_slope: float32 [3, 4, 32, 16, 128], P(None, None, 'gx', 'gy'), may hold values from -1 to 1, as said below
- embed_scale: float32 [100], replicated, may hold values from -12 to 12
- embed_bias: float32 [100], replicated, may hold values from -4 to 4
- desc_gain: float32 [1600], replicated, may hold values from 0.25 to 1.75
- fit_in: bfloat16 [128, 1600], replicated, may hold values from -0.15625 to 0.15625
- fit_bias: float32 [128], replicated, may hold values from -3 to 3
- fit_hidden: bfloat16 [128, 128], replicated, may hold values from -0.5 to 0.5
- fit_bias_two: float32 [128], replicated, may hold values from -3 to 3
- fit_out: float32 [128], replicated, may hold values from -0.5 to 0.5
Outputs:
- centroid_energy: float32 [32, 16, 128], P('gx', 'gy')
- centroid_force: float32 [3, 32, 16, 128], P(None, 'gx', 'gy')
Inputs may be any that keep to these rules, and one draw needn't show every extreme that they name: `live_count`: slots below a column's count are live; some column has all 128 slots live. `neighbours`: every entry names a live slot of one of the nine blocks of the column's neighbourhood. `stencil_base`: along x the base lies in -1 to 10, along y in -1 to 22, along z in 0 to 383. `positions`: x lies in 0 to 12, y in 0 to 24, z in 0 to 384. `spline_weight`: cubic B-spline weights of a fraction in [0, 1) for each axis; the four weights sum to one. `spline_slope`: the derivatives of those weights with respect to the fraction.
All inputs are finite; a program needn't handle non-finite values.
Results may differ from a plain program's by a relative error of at most 0.006.
The roundings to bfloat16 on the way count: a program that leaves them out, or rounds other values in their place, can miss the bound.
Values sent between devices are 32-bit elements; how exact they have to be, the bound alone decides.
No kernel may reach another device: no remote copies, remote signals or barrier semaphores. Data moves between devices by JAX's collectives and lax.ppermute only.
A program may use at most 64 MiB of HBM per device.

v0:
```python
import math

import jax
import jax.numpy as jnp
import numpy as np
from jax import lax
from jax.experimental import pallas as pl
from jax.experimental.pallas import tpu as pltpu
from jax.sharding import PartitionSpec as P

GRID = 384
AXIS = 16
ATOMS = 128
NEIGH = 32
EMB = 100
EMB_ROWS = 104
DESC = 1600
CX = 12
CY = 24
N_GX = 32
N_GY = 16
SLOTS = 24
LANES = 96
WIN = 256
HALF = 1024

radius_scale = 4.0
screen_width = 0.25
norm_floor = 1e-06
full_turn = 2.0 * math.pi
f32 = jnp.float32
bf16 = jnp.bfloat16


def axis_modes():
    freq = np.concatenate([np.arange(193), np.arange(1, 192)])
    is_sine = np.concatenate([np.zeros(193), np.ones(191)]).astype(np.int64)
    return freq, is_sine


def mode_table(cells):
    freq, is_sine = axis_modes()
    turn = (freq[:, None] * cells[None, :] - 96 * is_sine[:, None]) % GRID
    return np.cos(full_turn * turn / GRID)


def mode_weight(freq):
    return np.where((freq == 0) | (freq == GRID // 2), 1.0, 2.0) / GRID


def halves(table):
    table = table.astype(np.float32)
    upper = table.astype(jnp.bfloat16)
    lower = (table - upper.astype(np.float32)).astype(jnp.bfloat16)
    return upper, lower


FREQ, _ = axis_modes()
WAVE = full_turn / GRID
CELLS_X = (np.arange(N_GX)[:, None] * CX + np.arange(16)[None, :] - 1).reshape(-1) % GRID
CELLS_Y = (np.arange(2)[:, None] * 8 * CY + np.arange(WIN)[None, :] - 1).reshape(-1) % GRID
TABLE_X = mode_table(CELLS_X)
TABLE_Y = mode_table(CELLS_Y)
X_IN = halves(TABLE_X)
X_OUT = halves(TABLE_X.T)
Y_IN = halves(TABLE_Y.T)
Y_OUT = halves(TABLE_Y)
SQUARE_X = np.broadcast_to(((FREQ * WAVE) ** 2)[:, None], (GRID, 128)).astype(np.float32)
WEIGHT_X = np.broadcast_to(mode_weight(FREQ)[:, None], (GRID, 128)).astype(np.float32)
SQUARE_Y = np.zeros((4, 1, 128), np.float32)
SQUARE_Y[:, 0, :LANES] = ((FREQ * WAVE) ** 2).reshape(4, LANES)
WEIGHT_Y = np.zeros((4, 1, 128), np.float32)
WEIGHT_Y[:, 0, :LANES] = mode_weight(FREQ).reshape(4, LANES)


def split(value):
    upper = value.astype(bf16)
    return upper, (value - upper.astype(f32)).astype(bf16)


def product(left, right, dims=(((1,), (0,)), ((), ()))):
    a, b = left
    c, d = right
    dot = lambda x, y: lax.dot_general(x, y, dims, preferred_element_type=f32)
    return dot(a, c) + (dot(a, d) + dot(b, c))


def vmem(count):
    return [pl.BlockSpec(memory_space=pltpu.VMEM)] * count


SMEM = pl.BlockSpec(memory_space=pltpu.SMEM)
PARAMS = pltpu.CompilerParams(vmem_limit_bytes=48 * 1024 * 1024)


def charge_kernel(
    count, before, middle, after, listed, base, weight, packed, gain, fit_in, fit_hidden,
    sites, own, mixed, descriptor, normed,
):
    entry = listed[...]
    block = lax.shift_right_logical(entry, 7)
    slot = jnp.bitwise_and(entry, ATOMS - 1)
    picked = [jnp.zeros((NEIGH, ATOMS), f32) for _ in range(3)]
    for a, rows in enumerate((before, middle, after)):
        for b in range(3):
            here = block == a * 3 + b
            for c, shift in enumerate(((a - 1) * CX, (b - 1) * CY, 0)):
                row = rows[b * 3 + c : b * 3 + c + 1, :] + float(shift)
                row = jnp.broadcast_to(row, (NEIGH, ATOMS))
                value = jnp.take_along_axis(row, slot, axis=1)
                picked[c] = jnp.where(here, value, picked[c])
    delta = [picked[c] - middle[3 + c : 4 + c, :] for c in range(3)]
    radius = jnp.sqrt(delta[0] * delta[0] + delta[1] * delta[1] + delta[2] * delta[2])
    smooth = 1.0 / (1.0 + radius / radius_scale)
    factor = smooth / (radius + radius_scale)
    envelope = [smooth] + [d * factor for d in delta]

    columns = jnp.transpose(packed[...])
    column = lambda k, lo, hi: jnp.broadcast_to(columns[lo:hi, k : k + 1], (hi - lo, ATOMS))
    for lo, hi in ((0, 32), (32, 64), (64, EMB_ROWS)):
        scale, bias = column(0, lo, hi), column(1, lo, hi)
        total = [jnp.zeros((hi - lo, ATOMS), f32) for _ in range(4)]
        for k in range(NEIGH):
            embed = jnp.tanh(smooth[k : k + 1, :] * scale + bias)
            for c in range(4):
                total[c] = total[c] + embed * envelope[c][k : k + 1, :]
        for c in range(4):
            mixed[c, lo:hi, :] = total[c]
    second_factor = [mixed[c, 0:AXIS, :] for c in range(4)]
    squares = jnp.zeros((AXIS, ATOMS), f32)
    for e in range(EMB):
        value = mixed[0, e : e + 1, :] * second_factor[0]
        for c in range(1, 4):
            value = value + mixed[c, e : e + 1, :] * second_factor[c]
        squares = squares + value * value
        descriptor[e * AXIS : (e + 1) * AXIS, :] = value
    mean = jnp.sum(squares, axis=0, keepdims=True) * (1.0 / DESC)
    scaling = lax.rsqrt(mean + norm_floor)
    for e in range(EMB):
        rows = slice(e * AXIS, (e + 1) * AXIS)
        value = descriptor[rows, :] * scaling * jnp.broadcast_to(gain[rows, :], (AXIS, ATOMS))
        normed[rows, :] = value.astype(bf16)
    first = jnp.tanh(
        jnp.dot(fit_in[...], normed[...], preferred_element_type=f32) + column(2, 0, 128)
    )
    second = (
        jnp.tanh(
            jnp.dot(fit_hidden[...], first.astype(bf16), preferred_element_type=f32)
            + column(3, 0, 128)
        )
        + first
    )
    charge = jnp.sum(column(4, 0, 128) * second, axis=0, keepdims=True)
    place = lax.broadcasted_iota(jnp.int32, (1, ATOMS), 1)
    charge = jnp.where(place < count[0, 0], charge, 0.0)
    own[...] = charge
    fraction = weight[1] + 2.0 * weight[2] + 3.0 * weight[3] - 1.0
    record = jnp.concatenate(
        [base[...].astype(f32), fraction, charge, jnp.zeros((1, ATOMS), f32)], axis=0
    )
    for j in range(N_GY):
        sites[j] = record


def spline(fraction):
    remain = 1.0 - fraction
    square = fraction * fraction
    cube = square * fraction
    return [
        remain * remain * remain * (1.0 / 6.0),
        (3.0 * cube - 6.0 * square + 4.0) * (1.0 / 6.0),
        (-3.0 * cube + 3.0 * square + 3.0 * fraction + 1.0) * (1.0 / 6.0),
        cube * (1.0 / 6.0),
    ]


def spline_rate(fraction):
    remain = 1.0 - fraction
    square = fraction * fraction
    return [
        -0.5 * remain * remain,
        (3.0 * square - 4.0 * fraction) * 0.5,
        (-3.0 * square + 2.0 * fraction + 1.0) * 0.5,
        0.5 * square,
    ]


def tap_table(first, values, rows):
    away = lax.broadcasted_iota(jnp.int32, (rows, ATOMS), 0).astype(f32) - first
    total = jnp.zeros((rows, ATOMS), f32)
    for t, value in enumerate(values):
        total = jnp.where(away == float(t), value, total)
    return total


def cos_sin(step):
    step = step - GRID * jnp.round(step * (1.0 / GRID))
    quarter = jnp.round(step * (1.0 / 96.0))
    angle = (step - 96.0 * quarter) * WAVE
    square = angle * angle
    sine = angle * (
        1.0 + square * (-1.0 / 6 + square * (1.0 / 120 + square * (-1.0 / 5040 + square / 362880)))
    )
    cosine = 1.0 + square * (
        -0.5 + square * (1.0 / 24 + square * (-1.0 / 720 + square * (1.0 / 40320 - square / 3628800)))
    )
    odd = jnp.abs(quarter) == 1.0
    straight = jnp.where(jnp.abs(quarter) == 2.0, -1.0, 1.0)
    turned = jnp.where(odd, quarter, straight)
    cos_value = jnp.where(odd, -sine, cosine) * turned
    sin_value = jnp.where(odd, cosine, sine) * turned
    return cos_value, sin_value


def z_setup(device):
    row = lax.broadcasted_iota(jnp.int32, (SLOTS, ATOMS), 0)
    is_sine = row >= 12
    freq = (device * 12 + jnp.where(is_sine, row - 12, row)).astype(f32)
    phase = jnp.where(is_sine, 96.0, 0.0)
    turns = [cos_sin(freq * float(t)) for t in range(4)]
    return freq, phase, turns


def z_modes(setup, base, lists):
    freq, phase, turns = setup
    cosine, sine = cos_sin(freq * base - phase)
    out = []
    for values in lists:
        along = values[0] + sum(values[t] * turns[t][0] for t in range(1, 4))
        across = sum(values[t] * turns[t][1] for t in range(1, 4))
        out.append(cosine * along - sine * across)
    return out


def window(j):
    offset = CY * (j % 8)
    start = offset // 16 * 16
    return start, offset - start


def forward_kernel(device, sites, y_hi, y_lo, out, u_hi, u_lo, w_hi, w_lo, packed):
    setup = z_setup(device[0])
    w_hi[...] = jnp.zeros(w_hi.shape, bf16)
    w_lo[...] = jnp.zeros(w_lo.shape, bf16)
    total = None
    for half in range(2):
        for c in range(8):
            j = half * 8 + c
            lanes = slice(c * ATOMS, (c + 1) * ATOMS)
            row = lambda r: sites[j, r : r + 1, :]
            weight_x = [w * row(6) for w in spline(row(3))]
            table_x = tap_table(row(0) + 1.0, weight_x, 16)
            start, shift = window(j)
            table_y = tap_table(row(1) + (1.0 + shift), spline(row(4)), 48)
            hi, lo = split(table_y)
            w_hi[half, start : start + 48, lanes] = hi
            w_lo[half, start : start + 48, lanes] = lo
            (along_z,) = z_modes(setup, row(2), [spline(row(5))])
            for m in range(SLOTS):
                hi, lo = split(along_z[m : m + 1, :] * table_x)
                u_hi[half, m * 16 : (m + 1) * 16, lanes] = hi
                u_lo[half, m * 16 : (m + 1) * 16, lanes] = lo
        cells = product(
            (u_hi[half], u_lo[half]), (w_hi[half], w_lo[half]), (((1,), (1,)), ((), ()))
        )
        rows = slice(half * WIN, (half + 1) * WIN)
        part = product(split(cells), (y_hi[rows, :], y_lo[rows, :]))
        total = part if total is None else total + part
    packed[...] = total
    for kq in range(4):
        block = packed[:, kq * LANES : (kq + 1) * LANES]
        for sg in range(8):
            out[sg * 4 + kq, :, 0:LANES] = block[sg * 48 : sg * 48 + 36, :]
            for p in range(3):
                out[sg * 4 + kq, 12 * p : 12 * p + 12, LANES:128] = block[
                    sg * 48 + 36 : sg * 48 + 48, 32 * p : 32 * p + 32
                ]


def x_kernel(square, weight, sx, wx, in_hi, in_lo, out_hi, out_lo, got, out, held):
    for i in range(N_GX):
        rows = slice(i * 16, (i + 1) * 16)
        for q in range(2):
            held[rows, q * 128 : q * 128 + LANES] = got[i, 16 * q : 16 * q + 16, 0:LANES]
        lane = 2 * 128
        held[i * 16 : i * 16 + 4, lane : lane + LANES] = got[i, 32:36, 0:LANES]
        for p in range(3):
            held[i * 16 + 4 : i * 16 + 16, lane + 32 * p : lane + 32 * p + 32] = got[
                i, 12 * p : 12 * p + 12, LANES:128
            ]
    result = []
    for q in range(3):
        lanes = slice(q * 128, q * 128 + 128)
        place = lax.broadcasted_iota(jnp.int32, (N_GX * 16, 128), 1)
        cells = jnp.where(place < LANES, held[:, lanes], 0.0)
        modes = product((in_hi[...], in_lo[...]), split(cells))
        wave = sx[...] + square[q : q + 1, :]
        safe = jnp.where(wave > 0, wave, 1.0)
        green = 2.0 * full_turn * jnp.exp(-0.5 * screen_width * screen_width * wave) / safe
        green = jnp.where(wave > 0, green, 0.0)
        modes = modes * (green * (wx[...] * weight[q : q + 1, :]))
        result.append(product((out_hi[...], out_lo[...]), split(modes)))
    for q in range(3):
        held[:, q * 128 : q * 128 + 128] = result[q]
    for i in range(N_GX):
        rows = slice(i * 16, (i + 1) * 16)
        for q in range(2):
            out[i, 16 * q : 16 * q + 16, 0:LANES] = held[rows, q * 128 : q * 128 + LANES]
        lane = 2 * 128
        out[i, 32:36, 0:LANES] = held[i * 16 : i * 16 + 4, lane : lane + LANES]
        for p in range(3):
            out[i, 12 * p : 12 * p + 12, LANES:128] = held[
                i * 16 + 4 : i * 16 + 16, lane + 32 * p : lane + 32 * p + 32
            ]


def inverse_kernel(device, sites, y_hi, y_lo, got, out, modes, w_hi, w_lo, d_hi, d_lo, field, rate):
    setup = z_setup(device[0])
    for kq in range(4):
        lanes = slice(kq * LANES, (kq + 1) * LANES)
        for sg in range(8):
            row = sg * 48
            modes[row : row + 36, lanes] = got[sg * 4 + kq, :, 0:LANES]
            for p in range(3):
                modes[row + 36 : row + 48, kq * LANES + 32 * p : kq * LANES + 32 * p + 32] = got[
                    sg * 4 + kq, 12 * p : 12 * p + 12, LANES:128
                ]
    spectrum = split(modes[...])
    for ref in (w_hi, w_lo, d_hi, d_lo):
        ref[...] = jnp.zeros(ref.shape, bf16)
    for half in range(2):
        for c in range(8):
            j = half * 8 + c
            lanes = slice(c * ATOMS, (c + 1) * ATOMS)
            start, shift = window(j)
            first = sites[j, 1:2, :] + (1.0 + shift)
            fraction = sites[j, 4:5, :]
            for values, hi_ref, lo_ref in (
                (spline(fraction), w_hi, w_lo),
                (spline_rate(fraction), d_hi, d_lo),
            ):
                hi, lo = split(tap_table(first, values, 48))
                hi_ref[half, start : start + 48, lanes] = hi
                lo_ref[half, start : start + 48, lanes] = lo
        lanes = slice(half * WIN, (half + 1) * WIN)
        cells = split(product(spectrum, (y_hi[:, lanes], y_lo[:, lanes])))
        field[...] = product(cells, (w_hi[half], w_lo[half]))
        rate[...] = product(cells, (d_hi[half], d_lo[half]))
        for c in range(8):
            j = half * 8 + c
            lanes = slice(c * ATOMS, (c + 1) * ATOMS)
            row = lambda r: sites[j, r : r + 1, :]
            fraction_z = row(5)
            along, slant = z_modes(setup, row(2), [spline(fraction_z), spline_rate(fraction_z)])
            value = jnp.zeros((16, ATOMS), f32)
            over_z = jnp.zeros((16, ATOMS), f32)
            over_y = jnp.zeros((16, ATOMS), f32)
            for m in range(SLOTS):
                tile = field[m * 16 : (m + 1) * 16, lanes]
                value = value + along[m : m + 1, :] * tile
                over_z = over_z + slant[m : m + 1, :] * tile
                over_y = over_y + along[m : m + 1, :] * rate[m * 16 : (m + 1) * 16, lanes]
            table_x = tap_table(row(0) + 1.0, spline(row(3)), 16)
            rate_x = tap_table(row(0) + 1.0, spline_rate(row(3)), 16)
            gather = lambda x: jnp.sum(x, axis=0, keepdims=True)
            out[j] = jnp.concatenate(
                [
                    0.5 * gather(table_x * value),
                    -gather(rate_x * value),
                    -gather(table_x * over_y),
                    -gather(table_x * over_z),
                    jnp.zeros((4, ATOMS), f32),
                ],
                axis=0,
            )


def final_kernel(parts, own, energy, force):
    total = parts[0]
    for j in range(1, N_GY):
        total = total + parts[j]
    total = total * own[...]
    energy[...] = total[0:1, :]
    force[...] = total[1:4, :]


def shape(*dims):
    return jax.ShapeDtypeStruct(dims, f32)


def local(
    positions,
    neighbours,
    live_count,
    stencil_base,
    spline_weight,
    spline_slope,
    embed_scale,
    embed_bias,
    desc_gain,
    fit_in,
    fit_bias,
    fit_hidden,
    fit_bias_two,
    fit_out,
):
    ring = lambda axis, step: [
        (i, (i + step) % lax.axis_size(axis)) for i in range(lax.axis_size(axis))
    ]
    mine = positions.reshape(3, ATOMS)
    left = lax.ppermute(mine, "gy", ring("gy", 1))
    right = lax.ppermute(mine, "gy", ring("gy", -1))
    column = jnp.concatenate([left, mine, right], axis=0)
    before = lax.ppermute(column, "gx", ring("gx", 1))
    after = lax.ppermute(column, "gx", ring("gx", -1))

    widen = lambda v: jnp.pad(v, (0, 128 - v.shape[0]))
    none = jnp.zeros((128,), f32)
    packed = jnp.stack(
        [widen(embed_scale), widen(embed_bias), fit_bias, fit_bias_two, fit_out, none, none, none]
    )
    sites, own = pl.pallas_call(
        charge_kernel,
        name="charge",
        out_shape=(shape(N_GY, 8, ATOMS), shape(1, ATOMS)),
        in_specs=[SMEM] + vmem(10),
        out_specs=tuple(vmem(2)),
        scratch_shapes=[
            pltpu.VMEM((4, EMB_ROWS, ATOMS), f32),
            pltpu.VMEM((DESC, ATOMS), f32),
            pltpu.VMEM((DESC, ATOMS), bf16),
        ],
        compiler_params=PARAMS,
    )(
        live_count,
        before,
        column,
        after,
        neighbours.reshape(NEIGH, ATOMS),
        stencil_base.reshape(3, ATOMS),
        spline_weight.reshape(3, 4, ATOMS).transpose(1, 0, 2),
        packed,
        desc_gain.reshape(DESC, 1),
        fit_in,
        fit_hidden,
    )
    sites = lax.all_to_all(sites, "gy", 0, 0, tiled=True)

    device = lax.axis_index("gy").reshape(1)
    spread = pl.pallas_call(
        forward_kernel,
        name="forward",
        out_shape=shape(N_GX, 36, 128),
        in_specs=[SMEM] + vmem(3),
        out_specs=vmem(1)[0],
        scratch_shapes=[
            pltpu.VMEM((2, GRID, HALF), bf16),
            pltpu.VMEM((2, GRID, HALF), bf16),
            pltpu.VMEM((2, WIN, HALF), bf16),
            pltpu.VMEM((2, WIN, HALF), bf16),
            pltpu.VMEM((GRID, GRID), f32),
        ],
        compiler_params=PARAMS,
    )(device, sites, *Y_IN)
    spread = lax.all_to_all(spread, "gx", 0, 0, tiled=True)

    gx, gy = lax.axis_index("gx"), lax.axis_index("gy")
    slot = (gx // 4) * 3 + jnp.arange(3)
    freq_z = gy * 12 + slot % 12
    square_z = jnp.square(freq_z.astype(f32) * WAVE)
    weight_z = jnp.where(freq_z == 0, 1.0, 2.0) / GRID
    quarter = gx % 4
    square = square_z[:, None] + jnp.asarray(SQUARE_Y)[quarter]
    weight = weight_z[:, None] * jnp.asarray(WEIGHT_Y)[quarter]
    spread = pl.pallas_call(
        x_kernel,
        name="convolve",
        out_shape=shape(N_GX, 36, 128),
        in_specs=vmem(9),
        out_specs=vmem(1)[0],
        scratch_shapes=[pltpu.VMEM((N_GX * 16, GRID), f32)],
        compiler_params=PARAMS,
    )(square, weight, SQUARE_X, WEIGHT_X, *X_IN, *X_OUT, spread)
    spread = lax.all_to_all(spread, "gx", 0, 0, tiled=True)

    parts = pl.pallas_call(
        inverse_kernel,
        name="inverse",
        out_shape=shape(N_GY, 8, ATOMS),
        in_specs=[SMEM] + vmem(4),
        out_specs=vmem(1)[0],
        scratch_shapes=[
            pltpu.VMEM((GRID, GRID), f32),
            pltpu.VMEM((2, WIN, HALF), bf16),
            pltpu.VMEM((2, WIN, HALF), bf16),
            pltpu.VMEM((2, WIN, HALF), bf16),
            pltpu.VMEM((2, WIN, HALF), bf16),
            pltpu.VMEM((GRID, HALF), f32),
            pltpu.VMEM((GRID, HALF), f32),
        ],
        compiler_params=PARAMS,
    )(device, sites, *Y_OUT, spread)
    parts = lax.all_to_all(parts, "gy", 0, 0, tiled=True)
    energy, force = pl.pallas_call(
        final_kernel,
        name="finish",
        out_shape=(shape(1, ATOMS), shape(3, ATOMS)),
        in_specs=vmem(2),
        out_specs=tuple(vmem(2)),
        compiler_params=PARAMS,
    )(parts, own)
    return energy.reshape(1, 1, ATOMS), force.reshape(3, 1, 1, ATOMS)


def solution(mesh):
    placed = (
        P(None, "gx", "gy", None),
        P(None, "gx", "gy", None),
        P("gx", "gy"),
        P(None, "gx", "gy", None),
        P(None, None, "gx", "gy", None),
        P(None, None, "gx", "gy", None),
        P(),
        P(),
        P(),
        P(),
        P(),
        P(),
        P(),
        P(),
    )
    return jax.shard_map(
        local,
        mesh=mesh,
        in_specs=placed,
        out_specs=(P("gx", "gy", None), P(None, "gx", "gy", None)),
        check_vma=False,
    )
```

profile of v0, /device:TPU:1, one launch (start us, length us, event | category | flops | bytes accessed | tf_op | source)
XLA Modules:
  0.0 117.5 jit_solution(10184597401000529179)
XLA Ops:
  0.6 0.7 copy.41
  1.3 12.1 %collective-permute-start.1 = (f32[3,128]{1,0:T(4,128)S(1)}, f32[3,128]{1,0:T(4,128)S(1)}, u32[]{:S(2)}, u32[]{:S(2)}) collective-permute-start(f32[3,128]{1,0:T(4,128)S(1)} %bitcast.30), channel_id=1, source_target_pairs={{0,15},{1,0},{2,1},{3,2},{4,3},{5,4},{6,5},{7,6},{8,7},{9,8},{10,9... | collective-permute-start | bytes 4616 | tf_op jit(solution)/shard_map/ppermute | solution.py:412
  13.4 1.9 %collective-permute-start = (f32[3,128]{1,0:T(4,128)S(1)}, f32[3,128]{1,0:T(4,128)S(1)}, u32[]{:S(2)}, u32[]{:S(2)}) collective-permute-start(f32[3,128]{1,0:T(4,128)S(1)} %bitcast.31), channel_id=1, source_target_pairs={{0,1},{1,2},{2,3},{3,4},{4,5},{5,6},{6,7},{7,8},{8,9},{9,10},{10,1... | collective-permute-start | bytes 4616 | tf_op jit(solution)/shard_map/ppermute | solution.py:411
  15.3 0.0 collective-permute-done.1
  15.3 3.6 %collective-permute-done = f32[3,128]{1,0:T(4,128)S(1)} collective-permute-done((f32[3,128]{1,0:T(4,128)S(1)}, f32[3,128]{1,0:T(4,128)S(1)}, u32[]{:S(2)}, u32[]{:S(2)}) %collective-permute-start) | collective-permute-done | bytes 1568 | tf_op jit(solution)/shard_map/ppermute | solution.py:411
  18.9 0.0 copy-start.13
  19.0 4.0 %collective-permute-start.3 = (f32[9,128]{1,0:T(8,128)S(1)}, f32[9,128]{1,0:T(8,128)S(1)}, u32[]{:S(2)}, u32[]{:S(2)}) collective-permute-start(f32[9,128]{1,0:T(8,128)S(1)} %pad_maximum_fusion.middle), channel_id=1, source_target_pairs={{0,496},{16,0},{32,16},{48,32},{64,48},{80,64},{96,80},{112,96},{1... | collective-permute-start | bytes 13832 | tf_op jit(solution)/shard_map/ppermute | solution.py:415
  23.0 3.1 %collective-permute-start.2 = (f32[9,128]{1,0:T(8,128)S(1)}, f32[9,128]{1,0:T(8,128)S(1)}, u32[]{:S(2)}, u32[]{:S(2)}) collective-permute-start(f32[9,128]{1,0:T(8,128)S(1)} %pad_maximum_fusion.middle), channel_id=1, source_target_pairs={{0,16},{16,32},{32,48},{48,64},{64,80},{80,96},{96,112},{112,128},... | collective-permute-start | bytes 13832 | tf_op jit(solution)/shard_map/ppermute | solution.py:414
  26.1 0.0 copy-done.18
  26.1 0.0 copy-done.19
  26.8 0.0 copy-done.14
  26.8 0.0 copy-done.13
  26.8 0.0 copy-start.12
  26.8 1.2 %copy.32.fit_in = bf16[128,1600]{1,0:T(8,128)(2,1)S(1)} copy(bf16[128,1600]{0,1:T(8,128)(2,1)} %param.34) | data formatting | bytes 819200 | tf_op args[9]
  28.1 0.0 copy-done.12
  28.1 0.0 copy-start.15
  28.1 0.0 copy-start.16
  28.1 0.0 copy-start.17
  28.1 0.0 copy-start.10
  28.1 0.3 reshape.57.gain
  28.4 0.0 copy-start.11
  28.4 0.3 copy-done.15
  28.7 0.0 copy-done.16
  28.8 0.0 copy-done.17
  28.8 0.0 collective-permute-done.3.after
  28.8 0.0 collective-permute-done.2.before
  28.8 0.1 copy-done.10
  28.9 0.2 copy-done.11
  29.1 2.5 %charge.1 = (f32[16,8,128]{2,1,0:T(8,128)}, f32[1,128]{1,0:T(1,128)S(1)}) custom-call(s32[1,1]{1,0:T(1,128)S(6)} %copy.42.count, f32[9,128]{1,0:T(8,128)S(1)} %collective-permute-done.2.before, f32[9,128]{1,0:T(8,128)S(1)} %pad_maximum_fusion.middle, f32[9,128]{1,0:T(8,128)S(1)} %collective-permute-done.3.after, s32[32,128]{1,0:T(8,128)S(1)} %bitcast.27, ...), custom_call_target="tpu_custom_call" | custom-call | tf_op jit(solution)/shard_map/charge/pallas_call | solution.py:422
  31.6 5.5 %all-to-all-start = ((f32[16,8,128]{2,1,0:T(8,128)}), f32[16,8,128]{2,1,0:T(8,128)S(1)}, u32[]{:S(2)}, u32[]{:S(2)}) async-start(f32[16,8,128]{2,1,0:T(8,128)} %get-tuple-element.6), calls=%async_computation | async-start | bytes 131072 | tf_op jit(solution)/shard_map/all_to_all | solution.py:447
  37.2 11.6 %all-to-all-done.sites = f32[16,8,128]{2,1,0:T(8,128)S(1)} async-done(((f32[16,8,128]{2,1,0:T(8,128)}), f32[16,8,128]{2,1,0:T(8,128)S(1)}, u32[]{:S(2)}, u32[]{:S(2)}) %all-to-all-start) | async-done | bytes 65568 | tf_op jit(solution)/shard_map/all_to_all | solution.py:447
  48.7 0.0 copy-done.6
  48.7 0.0 copy-start.9
  48.7 5.1 %forward.1 = f32[32,36,128]{2,1,0:T(8,128)} custom-call(s32[1]{0:T(128)} %bitcast.device, f32[16,8,128]{2,1,0:T(8,128)S(1)} %all-to-all-done.sites, bf16[512,384]{1,0:T(8,128)(2,1)S(1)} %copy-done.7, bf16[512,384]{1,0:T(8,128)(2,1)S(1)} %copy-done.6), custom_call_target="tpu_custom_call" | custom-call | tf_op jit(solution)/shard_map/forward/pallas_call | solution.py:450
  53.9 10.8 %all-to-all-start.1 = ((f32[32,36,128]{2,1,0:T(8,128)}), f32[32,36,128]{2,1,0:T(8,128)S(1)}, u32[]{:S(2)}, u32[]{:S(2)}) async-start(f32[32,36,128]{2,1,0:T(8,128)} %forward.1), calls=%async_computation.1 | async-start | bytes 1310720 | tf_op jit(solution)/shard_map/all_to_all | solution.py:465
  64.7 0.7 dynamic-slice_bitcast_fusion
  65.4 0.1 broadcast_multiply_fusion.weight
  65.4 0.1 broadcast_add_fusion.square
  65.5 12.2 %all-to-all-done.1.got = f32[32,36,128]{2,1,0:T(8,128)S(1)} async-done(((f32[32,36,128]{2,1,0:T(8,128)}), f32[32,36,128]{2,1,0:T(8,128)S(1)}, u32[]{:S(2)}, u32[]{:S(2)}) %all-to-all-start.1) | async-done | bytes 589856 | tf_op jit(solution)/shard_map/all_to_all | solution.py:465
  77.7 3.0 %convolve.1 = f32[32,36,128]{2,1,0:T(8,128)S(1)} custom-call(f32[3,128]{1,0:T(4,128)S(1)} %broadcast_add_fusion.square, f32[3,128]{1,0:T(4,128)S(1)} %broadcast_multiply_fusion.weight, f32[384,128]{1,0:T(8,128)S(1)} %copy-done.9, f32[384,128]{1,0:T(8,128)S(1)} %copy-done.8, bf16[384,512]{1,0:T(8,128)(2,1)S(1)} %copy-done.3, bf16[384,512]{1,0:T(8,128)(2,1)S(1)} %copy-done.2, ...), custom_call_target="tpu_custom_call" | custom-call | tf_op jit(solution)/shard_map/convolve/pallas_call | solution.py:475
  80.7 0.0 copy-start.4
  80.8 0.0 copy-start.5
  80.8 16.5 %all_to_all.20.got = f32[32,36,128]{2,1,0:T(8,128)S(1)} all-to-all(f32[32,36,128]{2,1,0:T(8,128)S(1)} %convolve.1), channel_id=1, replica_groups=mesh['gx'=32,'gy'=16] {'gx'}, dimensions={0} | all-to-all | bytes 1179648 | tf_op jit(solution)/shard_map/all_to_all | solution.py:484
  97.3 0.0 copy-done.5
  97.3 4.9 %inverse.1 = f32[16,8,128]{2,1,0:T(8,128)S(1)} custom-call(s32[1]{0:T(128)} %bitcast.device, f32[16,8,128]{2,1,0:T(8,128)S(1)} %all-to-all-done.sites, bf16[384,512]{1,0:T(8,128)(2,1)S(1)} %copy-done.5, bf16[384,512]{1,0:T(8,128)(2,1)S(1)} %copy-done.4, f32[32,36,128]{2,1,0:T(8,128)S(1)} %all_to_all.20.got), custom_call_target="tpu_custom_call" | custom-call | tf_op jit(solution)/shard_map/inverse/pallas_call | solution.py:486
  102.2 14.2 %all_to_all.21.parts = f32[16,8,128]{2,1,0:T(8,128)S(1)} all-to-all(f32[16,8,128]{2,1,0:T(8,128)S(1)} %inverse.1), channel_id=1, replica_groups=mesh['gx'=32,'gy'=16] {'gy'}, dimensions={0} | all-to-all | bytes 131072 | tf_op jit(solution)/shard_map/all_to_all | solution.py:503
  116.5 0.5 finish.1
  117.0 0.6 copy.33
  (26 shorter events, 0.1 us)
Async XLA Ops:
  1.3 24.8 %copy-start.18 = (f32[100]{0:T(128)S(1)}, f32[100]{0:T(128)}, u32[]{:S(2)}) copy-start(f32[100]{0:T(128)} %param.32) | copy-start | bytes 1204
  1.3 24.8 %copy-start.19 = (f32[100]{0:T(128)S(1)}, f32[100]{0:T(128)}, u32[]{:S(2)}) copy-start(f32[100]{0:T(128)} %param.31) | copy-start | bytes 1204
  1.3 14.0 %collective-permute-start.1 = (f32[3,128]{1,0:T(4,128)S(1)}, f32[3,128]{1,0:T(4,128)S(1)}, u32[]{:S(2)}, u32[]{:S(2)}) collective-permute-start(f32[3,128]{1,0:T(4,128)S(1)} %bitcast.30), channel_id=1, source_target_pairs={{0,15},{1,0},{2,1},{3,2},{4,3},{5,4},{6,5},{7,6},{8,7},{9,8},{10,9... | collective-permute-start | bytes 4616 | tf_op jit(solution)/shard_map/ppermute | solution.py:412
  13.4 5.5 %collective-permute-start = (f32[3,128]{1,0:T(4,128)S(1)}, f32[3,128]{1,0:T(4,128)S(1)}, u32[]{:S(2)}, u32[]{:S(2)}) collective-permute-start(f32[3,128]{1,0:T(4,128)S(1)} %bitcast.31), channel_id=1, source_target_pairs={{0,1},{1,2},{2,3},{3,4},{4,5},{5,6},{6,7},{7,8},{8,9},{9,10},{10,1... | collective-permute-start | bytes 4616 | tf_op jit(solution)/shard_map/ppermute | solution.py:411
  18.9 7.8 %copy-start.14 = (s32[3,1,1,128]{3,2,1,0:T(1,128)S(1)}, s32[3,1,1,128]{3,2,1,0:T(1,128)}, u32[]{:S(2)}) copy-start(s32[3,1,1,128]{3,2,1,0:T(1,128)} %param.29) | copy-start | bytes 4612
  18.9 7.8 %copy-start.13 = (f32[3,4,1,1,128]{4,3,2,1,0:T(1,128)S(1)}, f32[3,4,1,1,128]{4,3,2,1,0:T(1,128)}, u32[]{:S(2)}) copy-start(f32[3,4,1,1,128]{4,3,2,1,0:T(1,128)} %param.30) | copy-start | bytes 18436
  19.0 9.8 %collective-permute-start.3 = (f32[9,128]{1,0:T(8,128)S(1)}, f32[9,128]{1,0:T(8,128)S(1)}, u32[]{:S(2)}, u32[]{:S(2)}) collective-permute-start(f32[9,128]{1,0:T(8,128)S(1)} %pad_maximum_fusion.middle), channel_id=1, source_target_pairs={{0,496},{16,0},{32,16},{48,32},{64,48},{80,64},{96,80},{112,96},{1... | collective-permute-start | bytes 13832 | tf_op jit(solution)/shard_map/ppermute | solution.py:415
  23.0 5.8 %collective-permute-start.2 = (f32[9,128]{1,0:T(8,128)S(1)}, f32[9,128]{1,0:T(8,128)S(1)}, u32[]{:S(2)}, u32[]{:S(2)}) collective-permute-start(f32[9,128]{1,0:T(8,128)S(1)} %pad_maximum_fusion.middle), channel_id=1, source_target_pairs={{0,16},{16,32},{32,48},{48,64},{64,80},{80,96},{96,112},{112,128},... | collective-permute-start | bytes 13832 | tf_op jit(solution)/shard_map/ppermute | solution.py:414
  26.8 1.3 %copy-start.12 = (f32[1600]{0:T(1024)S(1)}, f32[1600]{0:T(1024)}, u32[]{:S(2)}) copy-start(f32[1600]{0:T(1024)} %param.33) | copy-start | bytes 19204
  28.1 0.7 copy-start.15
  28.1 0.7 copy-start.16
  28.1 0.7 copy-start.17
  28.1 0.8 copy-start.10
  28.4 0.7 copy-start.11
  29.1 19.6 %copy-start.6 = (bf16[512,384]{1,0:T(8,128)(2,1)S(1)}, bf16[512,384]{1,0:T(8,128)(2,1)}, u32[]{:S(2)}) copy-start(bf16[512,384]{1,0:T(8,128)(2,1)} %constant.87.clone.y_lo) | copy-start | bytes 1179652
  29.1 19.6 %copy-start.7 = (bf16[512,384]{1,0:T(8,128)(2,1)S(1)}, bf16[512,384]{1,0:T(8,128)(2,1)}, u32[]{:S(2)}) copy-start(bf16[512,384]{1,0:T(8,128)(2,1)} %constant.86.clone.y_hi) | copy-start | bytes 1179652
  31.6 17.1 %all-to-all-start = ((f32[16,8,128]{2,1,0:T(8,128)}), f32[16,8,128]{2,1,0:T(8,128)S(1)}, u32[]{:S(2)}, u32[]{:S(2)}) async-start(f32[16,8,128]{2,1,0:T(8,128)} %get-tuple-element.6), calls=%async_computation | async-start | bytes 131072 | tf_op jit(solution)/shard_map/all_to_all | solution.py:447
  48.7 29.0 %copy-start.3 = (bf16[384,512]{1,0:T(8,128)(2,1)S(1)}, bf16[384,512]{1,0:T(8,128)(2,1)}, u32[]{:S(2)}) copy-start(bf16[384,512]{1,0:T(8,128)(2,1)} %constant.92.clone.in_hi) | copy-start | bytes 1179652
  48.7 29.0 %copy-start.8 = (f32[384,128]{1,0:T(8,128)S(1)}, f32[384,128]{1,0:T(8,128)}, u32[]{:S(2)}) copy-start(f32[384,128]{1,0:T(8,128)} %constant.91.clone.wx) | copy-start | bytes 589828
  48.7 29.0 %copy-start.9 = (f32[384,128]{1,0:T(8,128)S(1)}, f32[384,128]{1,0:T(8,128)}, u32[]{:S(2)}) copy-start(f32[384,128]{1,0:T(8,128)} %constant.90.clone.sx) | copy-start | bytes 589828
  53.8 23.9 %copy-start = (bf16[512,384]{1,0:T(8,128)(2,1)S(1)}, bf16[512,384]{1,0:T(8,128)(2,1)}, u32[]{:S(2)}) copy-start(bf16[512,384]{1,0:T(8,128)(2,1)} %constant.95.clone.out_lo) | copy-start | bytes 1179652
  53.9 23.9 %copy-start.1 = (bf16[512,384]{1,0:T(8,128)(2,1)S(1)}, bf16[512,384]{1,0:T(8,128)(2,1)}, u32[]{:S(2)}) copy-start(bf16[512,384]{1,0:T(8,128)(2,1)} %constant.94.clone.out_hi) | copy-start | bytes 1179652
  53.9 23.9 %copy-start.2 = (bf16[384,512]{1,0:T(8,128)(2,1)S(1)}, bf16[384,512]{1,0:T(8,128)(2,1)}, u32[]{:S(2)}) copy-start(bf16[384,512]{1,0:T(8,128)(2,1)} %constant.93.clone.in_lo) | copy-start | bytes 1179652
  53.9 23.8 %all-to-all-start.1 = ((f32[32,36,128]{2,1,0:T(8,128)}), f32[32,36,128]{2,1,0:T(8,128)S(1)}, u32[]{:S(2)}, u32[]{:S(2)}) async-start(f32[32,36,128]{2,1,0:T(8,128)} %forward.1), calls=%async_computation.1 | async-start | bytes 1310720 | tf_op jit(solution)/shard_map/all_to_all | solution.py:465
  80.7 16.6 %copy-start.4 = (bf16[384,512]{1,0:T(8,128)(2,1)S(1)}, bf16[384,512]{1,0:T(8,128)(2,1)}, u32[]{:S(2)}) copy-start(bf16[384,512]{1,0:T(8,128)(2,1)} %constant.97.clone.y_lo) | copy-start | bytes 1179652
  80.8 16.6 %copy-start.5 = (bf16[384,512]{1,0:T(8,128)(2,1)S(1)}, bf16[384,512]{1,0:T(8,128)(2,1)}, u32[]{:S(2)}) copy-start(bf16[384,512]{1,0:T(8,128)(2,1)} %constant.96.clone.y_hi) | copy-start | bytes 1179652
where the time goes:
time: 118 us
  starting transfers between devices  37.4 us (32%)
  blocking collectives  30.8 us (26%)
  waiting for transfers between devices  27.3 us (23%)
  Pallas kernels  16 us (14%)
  local copies, waits for them, and re-layouts  4.22 us (4%)
  between operations  1.61 us (1%)
    all_to_all x1, blocking collectives, local(): spread = lax.all_to_all(spread, 'gx', 0, 0, tiled=True)  16.5 us
    all_to_all x1, blocking collectives, local(): parts = lax.all_to_all(parts, 'gy', 0, 0, tiled=True)  14.2 us
    all_to_all x1, waiting for transfers between devices, local(): spread = lax.all_to_all(spread, 'gx', 0, 0, tiled=True)  12.2 us
    ppermute x1, starting transfers between devices, local(): right = lax.ppermute(mine, 'gy', ring('gy', -1))  12.1 us
    all_to_all x1, waiting for transfers between devices, local(): sites = lax.all_to_all(sites, 'gy', 0, 0, tiled=True)  11.6 us
    all_to_all x1, starting transfers between devices, local(): spread = lax.all_to_all(spread, 'gx', 0, 0, tiled=True)  10.8 us
    all_to_all x1, starting transfers between devices, local(): sites = lax.all_to_all(sites, 'gy', 0, 0, tiled=True)  5.53 us
    pallas_call x1, Pallas kernels, local(): pl.pallas_call(forward_kernel, name='forward', out_shape=shape(N_GX, 36,...  5.1 us
  transfers between devices with their start and end apart: 6, of which 3 were waited for; matrix products, arithmetic and copies ran while one was open for 2% of the time, Pallas kernels for 0%

commit v1 on v0

v1 whole, which is shorter than its diff:
```python
import math

import jax
import jax.numpy as jnp
import numpy as np
from jax import lax
from jax.experimental import pallas as pl
from jax.experimental.pallas import tpu as pltpu
from jax.sharding import PartitionSpec as P

GRID = 384
AXIS = 16
ATOMS = 128
NEIGH = 32
EMB = 100
EMB_ROWS = 104
DESC = 1600
CX = 12
CY = 24
N_GX = 32
N_GY = 16
SLOTS = 24
LANES = 96
WIN = 64
PAIR = 256

radius_scale = 4.0
screen_width = 0.25
norm_floor = 1e-06
full_turn = 2.0 * math.pi
f32 = jnp.float32
bf16 = jnp.bfloat16


def axis_modes():
    cosines = [(k, 0) for k in range(193)]
    sines = [(k, 1) for k in range(1, 192)]
    modes = [m for odd in (0, 1) for m in cosines + sines if m[0] % 2 == odd]
    return np.array([k for k, _ in modes]), np.array([kind for _, kind in modes])


FREQ, IS_SINE = axis_modes()
WAVE = full_turn / GRID
SIDE = GRID // 2


def mode_table(cells):
    turn = (FREQ[:, None] * cells[None, :] - 96 * IS_SINE[:, None]) % GRID
    return np.cos(full_turn * turn / GRID)


def mode_weight(freq):
    return np.where((freq == 0) | (freq == GRID // 2), 1.0, 2.0) / GRID


def halves(table):
    table = table.astype(np.float32)
    upper = table.astype(jnp.bfloat16)
    lower = (table - upper.astype(np.float32)).astype(jnp.bfloat16)
    return upper, lower


def by_parity(table, stacked):
    out = []
    for part in (table[:SIDE], table[SIDE:]):
        pair = halves(part.T if stacked == "columns" else part)
        out.append(np.concatenate(pair, axis=0) if stacked != "none" else pair)
    return out


CELLS_X = (np.arange(16)[:, None] * CX + np.arange(16)[None, :] - 1).reshape(-1) % GRID
CELLS_Y = (np.arange(4)[:, None] * 2 * CY + np.arange(64)[None, :] - 1).reshape(-1) % GRID
TABLE_X = mode_table(CELLS_X)
TABLE_Y = mode_table(CELLS_Y)
X_IN = by_parity(TABLE_X, "rows")
X_OUT = by_parity(TABLE_X, "columns")
Y_IN = by_parity(TABLE_Y, "columns")
Y_OUT = by_parity(TABLE_Y, "rows")
SQUARE_X = np.broadcast_to(((FREQ * WAVE) ** 2)[:, None], (GRID, 128)).astype(np.float32)
WEIGHT_X = np.broadcast_to(mode_weight(FREQ)[:, None], (GRID, 128)).astype(np.float32)
SQUARE_Y = np.zeros((4, 1, 128), np.float32)
SQUARE_Y[:, 0, :LANES] = ((FREQ * WAVE) ** 2).reshape(4, LANES)
WEIGHT_Y = np.zeros((4, 1, 128), np.float32)
WEIGHT_Y[:, 0, :LANES] = mode_weight(FREQ).reshape(4, LANES)


def split(value):
    upper = value.astype(bf16)
    return upper, (value - upper.astype(f32)).astype(bf16)


def product(left, right, dims=(((1,), (0,)), ((), ()))):
    a, b = left
    c, d = right
    dot = lambda x, y: lax.dot_general(x, y, dims, preferred_element_type=f32)
    return dot(a, c) + (dot(a, d) + dot(b, c))


def vmem(count):
    return [pl.BlockSpec(memory_space=pltpu.VMEM)] * count


SMEM = pl.BlockSpec(memory_space=pltpu.SMEM)
PARAMS = pltpu.CompilerParams(vmem_limit_bytes=48 * 1024 * 1024)


def charge_kernel(
    count, before, middle, after, listed, base, weight, scale, bias, bias_one, bias_two, read_out,
    gain, fit_in, fit_hidden, sites, own, vectors, mixed, descriptor, normed,
):
    vectors[0:1, 0:EMB] = scale[...]
    vectors[1:2, 0:EMB] = bias[...]
    for k, ref in enumerate((bias_one, bias_two, read_out)):
        vectors[k + 2 : k + 3, :] = ref[...]
    entry = listed[...]
    block = lax.shift_right_logical(entry, 7)
    slot = jnp.bitwise_and(entry, ATOMS - 1)
    picked = [jnp.zeros((NEIGH, ATOMS), f32) for _ in range(3)]
    for a, rows in enumerate((before, middle, after)):
        for b in range(3):
            here = block == a * 3 + b
            for c, shift in enumerate(((a - 1) * CX, (b - 1) * CY, 0)):
                row = rows[b * 3 + c, 0] + float(shift)
                row = jnp.broadcast_to(row, (NEIGH, ATOMS))
                value = jnp.take_along_axis(row, slot, axis=1)
                picked[c] = jnp.where(here, value, picked[c])
    delta = [picked[c] - middle[3 + c, 0] for c in range(3)]
    radius = jnp.sqrt(delta[0] * delta[0] + delta[1] * delta[1] + delta[2] * delta[2])
    smooth = 1.0 / (1.0 + radius / radius_scale)
    factor = smooth / (radius + radius_scale)
    envelope = [smooth] + [d * factor for d in delta]

    columns = jnp.transpose(vectors[...])
    column = lambda k, lo, hi: jnp.broadcast_to(columns[lo:hi, k : k + 1], (hi - lo, ATOMS))
    for lo, hi in ((0, 32), (32, 64), (64, EMB_ROWS)):
        scale, bias = column(0, lo, hi), column(1, lo, hi)
        total = [jnp.zeros((hi - lo, ATOMS), f32) for _ in range(4)]
        for k in range(NEIGH):
            embed = jnp.tanh(smooth[k : k + 1, :] * scale + bias)
            for c in range(4):
                total[c] = total[c] + embed * envelope[c][k : k + 1, :]
        for c in range(4):
            mixed[c, lo:hi, :] = total[c]
    second_factor = [mixed[c, 0:AXIS, :] for c in range(4)]
    squares = jnp.zeros((AXIS, ATOMS), f32)
    for e in range(EMB):
        value = mixed[0, e : e + 1, :] * second_factor[0]
        for c in range(1, 4):
            value = value + mixed[c, e : e + 1, :] * second_factor[c]
        squares = squares + value * value
        descriptor[e * AXIS : (e + 1) * AXIS, :] = value
    mean = jnp.sum(squares, axis=0, keepdims=True) * (1.0 / DESC)
    scaling = lax.rsqrt(mean + norm_floor)
    for e in range(EMB):
        rows = slice(e * AXIS, (e + 1) * AXIS)
        value = descriptor[rows, :] * scaling * jnp.broadcast_to(gain[rows, :], (AXIS, ATOMS))
        normed[rows, :] = value.astype(bf16)
    first = jnp.tanh(
        lax.dot_general(
            fit_in[...], normed[...], (((0,), (0,)), ((), ())), preferred_element_type=f32
        )
        + column(2, 0, 128)
    )
    second = (
        jnp.tanh(
            jnp.dot(fit_hidden[...], first.astype(bf16), preferred_element_type=f32)
            + column(3, 0, 128)
        )
        + first
    )
    charge = jnp.sum(column(4, 0, 128) * second, axis=0, keepdims=True)
    place = lax.broadcasted_iota(jnp.int32, (1, ATOMS), 1)
    charge = jnp.where(place < count[0, 0], charge, 0.0)
    own[0] = charge
    cell = [base[c, 0].astype(f32) for c in range(3)]
    fraction = [
        weight[c, 1, 0] + 2.0 * weight[c, 2, 0] + 3.0 * weight[c, 3, 0] - 1.0 for c in range(3)
    ]
    record = jnp.concatenate(cell + fraction + [charge, jnp.zeros((1, ATOMS), f32)], axis=0)
    for j in range(N_GY):
        sites[j] = record


def spline(fraction):
    remain = 1.0 - fraction
    square = fraction * fraction
    cube = square * fraction
    return [
        remain * remain * remain * (1.0 / 6.0),
        (3.0 * cube - 6.0 * square + 4.0) * (1.0 / 6.0),
        (-3.0 * cube + 3.0 * square + 3.0 * fraction + 1.0) * (1.0 / 6.0),
        cube * (1.0 / 6.0),
    ]


def spline_rate(fraction):
    remain = 1.0 - fraction
    square = fraction * fraction
    return [
        -0.5 * remain * remain,
        (3.0 * square - 4.0 * fraction) * 0.5,
        (-3.0 * square + 2.0 * fraction + 1.0) * 0.5,
        0.5 * square,
    ]


def tap_table(first, values, rows):
    away = lax.broadcasted_iota(jnp.int32, (rows, ATOMS), 0).astype(f32) - first
    total = jnp.zeros((rows, ATOMS), f32)
    for t, value in enumerate(values):
        total = jnp.where(away == float(t), value, total)
    return total


def cos_sin(step):
    step = step - GRID * jnp.round(step * (1.0 / GRID))
    quarter = jnp.round(step * (1.0 / 96.0))
    angle = (step - 96.0 * quarter) * WAVE
    square = angle * angle
    sine = angle * (
        1.0 + square * (-1.0 / 6 + square * (1.0 / 120 + square * (-1.0 / 5040 + square / 362880)))
    )
    cosine = 1.0 + square * (
        -0.5 + square * (1.0 / 24 + square * (-1.0 / 720 + square * (1.0 / 40320 - square / 3628800)))
    )
    odd = jnp.abs(quarter) == 1.0
    straight = jnp.where(jnp.abs(quarter) == 2.0, -1.0, 1.0)
    turned = jnp.where(odd, quarter, straight)
    cos_value = jnp.where(odd, -sine, cosine) * turned
    sin_value = jnp.where(odd, cosine, sine) * turned
    return cos_value, sin_value


def z_setup(device):
    row = lax.broadcasted_iota(jnp.int32, (SLOTS, ATOMS), 0)
    is_sine = row >= 12
    freq = (device * 12 + jnp.where(is_sine, row - 12, row)).astype(f32)
    phase = jnp.where(is_sine, 96.0, 0.0)
    turns = [cos_sin(freq * float(t)) for t in range(4)]
    return freq, phase, turns


def z_modes(setup, base, lists):
    freq, phase, turns = setup
    cosine, sine = cos_sin(freq * base - phase)
    out = []
    for values in lists:
        along = values[0] + sum(values[t] * turns[t][0] for t in range(1, 4))
        across = sum(values[t] * turns[t][1] for t in range(1, 4))
        out.append(cosine * along - sine * across)
    return out


def pair_table(sites, j, values):
    first = sites[j, 1:2, :] + (1.0 + CY * (j % 2))
    lo, hi = (0, 32) if j % 2 == 0 else (16, 64)
    table = tap_table(first - float(lo), values, hi - lo)
    pieces = [jnp.zeros((lo, ATOMS), f32)] if lo else []
    pieces.append(table)
    if hi < WIN:
        pieces.append(jnp.zeros((WIN - hi, ATOMS), f32))
    return split(jnp.concatenate(pieces, axis=0))


def first_half():
    return lax.broadcasted_iota(jnp.int32, (GRID, 128), 1) < WIN


def forward_kernel(device, sites, even, odd, out, u_hi, u_lo, w, held):
    setup = z_setup(device[0])
    cells = []
    for pair in range(8):
        for c in range(2):
            j = pair * 2 + c
            lanes = slice(c * ATOMS, (c + 1) * ATOMS)
            row = lambda r: sites[j, r : r + 1, :]
            weight_x = [v * row(6) for v in spline(row(3))]
            table_x = tap_table(row(0) + 1.0, weight_x, 16)
            hi, lo = pair_table(sites, j, spline(row(4)))
            w[pair, 0:WIN, lanes] = hi
            w[pair, WIN:, lanes] = lo
            (along_z,) = z_modes(setup, row(2), [spline(row(5))])
            for m in range(SLOTS):
                hi, lo = split(along_z[m : m + 1, :] * table_x)
                u_hi[pair, m * 16 : (m + 1) * 16, lanes] = hi
                u_lo[pair, m * 16 : (m + 1) * 16, lanes] = lo
        dims = (((1,), (1,)), ((), ()))
        both = lax.dot_general(u_hi[pair], w[pair], dims, preferred_element_type=f32)
        both = both + lax.dot_general(u_lo[pair], w[pair], dims, preferred_element_type=f32)
        cells.append(both + pltpu.roll(both, WIN, 1))
    front = first_half()
    tiles = [jnp.where(front, cells[2 * t], cells[2 * t + 1]) for t in range(4)]
    for parity, table in enumerate((even, odd)):
        sign = 1.0 - 2.0 * parity
        near = jnp.concatenate([tiles[0] + sign * tiles[2], tiles[1] + sign * tiles[3]], axis=1)
        held[...] = product(split(near), (table[0:256, :], table[256:512, :]))
        for side in range(2):
            kq = parity * 2 + side
            block = held[:, side * LANES : (side + 1) * LANES]
            for sg in range(8):
                out[sg * 4 + kq, :, 0:LANES] = block[sg * 48 : sg * 48 + 36, :]
                for p in range(3):
                    out[sg * 4 + kq, 12 * p : 12 * p + 12, LANES:128] = block[
                        sg * 48 + 36 : sg * 48 + 48, 32 * p : 32 * p + 32
                    ]


def x_kernel(square, weight, sx, wx, in_even, in_odd, out_even, out_odd, got, out, held):
    for i in range(N_GX):
        rows = slice(i * 16, (i + 1) * 16)
        for q in range(2):
            held[rows, q * 128 : q * 128 + LANES] = got[i, 16 * q : 16 * q + 16, 0:LANES]
        lane = 2 * 128
        held[i * 16 : i * 16 + 4, lane : lane + LANES] = got[i, 32:36, 0:LANES]
        for p in range(3):
            held[i * 16 + 4 : i * 16 + 16, lane + 32 * p : lane + 32 * p + 32] = got[
                i, 12 * p : 12 * p + 12, LANES:128
            ]
    dot = lambda x, y: jnp.dot(x, y, preferred_element_type=f32)
    near, far = held[0:256, :], held[256:512, :]
    result = []
    for parity, (table_in, table_out) in enumerate(((in_even, out_even), (in_odd, out_odd))):
        hi, lo = split(near + far if parity == 0 else near - far)
        both = dot(table_in[...], hi)
        modes = both[0:SIDE, :] + (both[SIDE:, :] + dot(table_in[0:SIDE, :], lo))
        rows = slice(parity * SIDE, (parity + 1) * SIDE)
        scaled = []
        for q in range(3):
            wave = sx[rows, :] + square[q : q + 1, :]
            safe = jnp.where(wave > 0, wave, 1.0)
            green = 2.0 * full_turn * jnp.exp(-0.5 * screen_width * screen_width * wave) / safe
            green = jnp.where(wave > 0, green, 0.0) * (wx[rows, :] * weight[q : q + 1, :])
            scaled.append(modes[:, q * 128 : (q + 1) * 128] * green)
        hi, lo = split(jnp.concatenate(scaled, axis=1))
        both = dot(table_out[...], hi)
        result.append(both[0:256, :] + (both[256:, :] + dot(table_out[0:256, :], lo)))
    held[0:256, :] = result[0] + result[1]
    held[256:512, :] = result[0] - result[1]
    for i in range(N_GX):
        rows = slice(i * 16, (i + 1) * 16)
        for q in range(2):
            out[i, 16 * q : 16 * q + 16, 0:LANES] = held[rows, q * 128 : q * 128 + LANES]
        lane = 2 * 128
        out[i, 32:36, 0:LANES] = held[i * 16 : i * 16 + 4, lane : lane + LANES]
        for p in range(3):
            out[i, 12 * p : 12 * p + 12, LANES:128] = held[
                i * 16 + 4 : i * 16 + 16, lane + 32 * p : lane + 32 * p + 32
            ]


def inverse_kernel(device, sites, even, odd, got, out, modes, w, d, field, rate):
    setup = z_setup(device[0])
    for kq in range(4):
        part, side = kq // 2, (kq % 2) * LANES
        for sg in range(8):
            row = sg * 48
            modes[part, row : row + 36, side : side + LANES] = got[sg * 4 + kq, :, 0:LANES]
            for p in range(3):
                modes[part, row + 36 : row + 48, side + 32 * p : side + 32 * p + 32] = got[
                    sg * 4 + kq, 12 * p : 12 * p + 12, LANES:128
                ]
    parts = [
        product(split(modes[p]), (table[0:SIDE, :], table[SIDE:, :]))
        for p, table in enumerate((even, odd))
    ]
    halves_y = [parts[0] + parts[1], parts[0] - parts[1]]
    front = first_half()
    for half in range(2):
        for tile in range(2):
            cells = halves_y[half][:, tile * 128 : (tile + 1) * 128]
            turned = pltpu.roll(cells, WIN, 1)
            for p, (near, far) in enumerate(((cells, turned), (turned, cells))):
                pair = half * 4 + tile * 2 + p
                upper = near.astype(bf16).astype(f32)
                lower = far - far.astype(bf16).astype(f32)
                mixed = jnp.where(front, upper, lower).astype(bf16)
                mixed = jnp.concatenate([mixed, mixed], axis=1)
                for c in range(2):
                    j = pair * 2 + c
                    lanes = slice(c * ATOMS, (c + 1) * ATOMS)
                    fraction = sites[j, 4:5, :]
                    for values, ref in ((spline(fraction), w), (spline_rate(fraction), d)):
                        hi, lo = pair_table(sites, j, values)
                        ref[pair, 0:WIN, lanes] = hi
                        ref[pair, WIN : 2 * WIN, lanes] = hi
                        ref[pair, 2 * WIN : 3 * WIN, lanes] = lo
                        ref[pair, 3 * WIN :, lanes] = lo
                field[pair % 2] = jnp.dot(mixed, w[pair], preferred_element_type=f32)
                rate[pair % 2] = jnp.dot(mixed, d[pair], preferred_element_type=f32)
                for c in range(2):
                    j = pair * 2 + c
                    lanes = slice(c * ATOMS, (c + 1) * ATOMS)
                    row = lambda r: sites[j, r : r + 1, :]
                    taps_z = [spline(row(5)), spline_rate(row(5))]
                    along, slant = z_modes(setup, row(2), taps_z)
                    value = jnp.zeros((16, ATOMS), f32)
                    over_z = jnp.zeros((16, ATOMS), f32)
                    over_y = jnp.zeros((16, ATOMS), f32)
                    for m in range(SLOTS):
                        rows = slice(m * 16, (m + 1) * 16)
                        here = field[pair % 2, rows, lanes]
                        value = value + along[m : m + 1, :] * here
                        over_z = over_z + slant[m : m + 1, :] * here
                        over_y = over_y + along[m : m + 1, :] * rate[pair % 2, rows, lanes]
                    table_x = tap_table(row(0) + 1.0, spline(row(3)), 16)
                    rate_x = tap_table(row(0) + 1.0, spline_rate(row(3)), 16)
                    gather = lambda x: jnp.sum(x, axis=0, keepdims=True)
                    out[j] = jnp.concatenate(
                        [
                            0.5 * gather(table_x * value),
                            -gather(rate_x * value),
                            -gather(table_x * over_y),
                            -gather(table_x * over_z),
                            jnp.zeros((4, ATOMS), f32),
                        ],
                        axis=0,
                    )


def final_kernel(parts, own, energy, force):
    total = parts[0]
    for j in range(1, N_GY):
        total = total + parts[j]
    total = total * own[0]
    energy[0] = total[0:1, :]
    for c in range(3):
        force[c, 0] = total[c + 1 : c + 2, :]


def shape(*dims):
    return jax.ShapeDtypeStruct(dims, f32)


def local(
    positions,
    neighbours,
    live_count,
    stencil_base,
    spline_weight,
    spline_slope,
    embed_scale,
    embed_bias,
    desc_gain,
    fit_in,
    fit_bias,
    fit_hidden,
    fit_bias_two,
    fit_out,
):
    ring = lambda axis, step: [
        (i, (i + step) % lax.axis_size(axis)) for i in range(lax.axis_size(axis))
    ]
    left = lax.ppermute(positions, "gy", ring("gy", 1))
    right = lax.ppermute(positions, "gy", ring("gy", -1))
    column = jnp.concatenate([left, positions, right], axis=0)
    before = lax.ppermute(column, "gx", ring("gx", 1))
    after = lax.ppermute(column, "gx", ring("gx", -1))

    gx, gy = lax.axis_index("gx"), lax.axis_index("gy")
    device = gy.reshape(1)
    slot = (gx // 4) * 3 + jnp.arange(3)
    freq_z = gy * 12 + slot % 12
    square_z = jnp.square(freq_z.astype(f32) * WAVE)
    weight_z = jnp.where(freq_z == 0, 1.0, 2.0) / GRID
    quarter = gx % 4
    square = square_z[:, None] + jnp.asarray(SQUARE_Y)[quarter]
    weight = weight_z[:, None] * jnp.asarray(WEIGHT_Y)[quarter]
    middle, gain, device, square, weight = lax.optimization_barrier(
        (column, desc_gain.reshape(DESC, 1), device, square, weight)
    )
    sites, own = pl.pallas_call(
        charge_kernel,
        name="charge",
        out_shape=(shape(N_GY, 8, ATOMS), shape(1, 1, ATOMS)),
        in_specs=[SMEM] + vmem(14),
        out_specs=tuple(vmem(2)),
        scratch_shapes=[
            pltpu.VMEM((8, ATOMS), f32),
            pltpu.VMEM((4, EMB_ROWS, ATOMS), f32),
            pltpu.VMEM((DESC, ATOMS), f32),
            pltpu.VMEM((DESC, ATOMS), bf16),
        ],
        compiler_params=PARAMS,
    )(
        live_count,
        before,
        middle,
        after,
        neighbours.reshape(NEIGH, ATOMS),
        stencil_base.reshape(3, 1, 1, ATOMS),
        spline_weight,
        embed_scale.reshape(1, EMB),
        embed_bias.reshape(1, EMB),
        fit_bias.reshape(1, 128),
        fit_bias_two.reshape(1, 128),
        fit_out.reshape(1, 128),
        gain,
        fit_in.T,
        fit_hidden,
    )
    sites = lax.all_to_all(sites, "gy", 0, 0, tiled=True)

    spread = pl.pallas_call(
        forward_kernel,
        name="forward",
        out_shape=shape(N_GX, 36, 128),
        in_specs=[SMEM] + vmem(3),
        out_specs=vmem(1)[0],
        scratch_shapes=[
            pltpu.VMEM((8, GRID, PAIR), bf16),
            pltpu.VMEM((8, GRID, PAIR), bf16),
            pltpu.VMEM((8, 2 * WIN, PAIR), bf16),
            pltpu.VMEM((GRID, SIDE), f32),
        ],
        compiler_params=PARAMS,
    )(device, sites, *Y_IN)
    spread = lax.all_to_all(spread, "gx", 0, 0, tiled=True)

    spread = pl.pallas_call(
        x_kernel,
        name="convolve",
        out_shape=shape(N_GX, 36, 128),
        in_specs=vmem(9),
        out_specs=vmem(1)[0],
        scratch_shapes=[pltpu.VMEM((N_GX * 16, GRID), f32)],
        compiler_params=PARAMS,
    )(square, weight, SQUARE_X, WEIGHT_X, *X_IN, *X_OUT, spread)
    spread = lax.all_to_all(spread, "gx", 0, 0, tiled=True)

    parts = pl.pallas_call(
        inverse_kernel,
        name="inverse",
        out_shape=shape(N_GY, 8, ATOMS),
        in_specs=[SMEM] + vmem(4),
        out_specs=vmem(1)[0],
        scratch_shapes=[
            pltpu.VMEM((2, GRID, SIDE), f32),
            pltpu.VMEM((8, 4 * WIN, PAIR), bf16),
            pltpu.VMEM((8, 4 * WIN, PAIR), bf16),
            pltpu.VMEM((2, GRID, PAIR), f32),
            pltpu.VMEM((2, GRID, PAIR), f32),
        ],
        compiler_params=PARAMS,
    )(device, sites, *Y_OUT, spread)
    parts = lax.all_to_all(parts, "gy", 0, 0, tiled=True)
    energy, force = pl.pallas_call(
        final_kernel,
        name="finish",
        out_shape=(shape(1, 1, ATOMS), shape(3, 1, 1, ATOMS)),
        in_specs=vmem(2),
        out_specs=tuple(vmem(2)),
        compiler_params=PARAMS,
    )(parts, own)
    return energy, force


def solution(mesh):
    placed = (
        P(None, "gx", "gy", None),
        P(None, "gx", "gy", None),
        P("gx", "gy"),
        P(None, "gx", "gy", None),
        P(None, None, "gx", "gy", None),
        P(None, None, "gx", "gy", None),
        P(),
        P(),
        P(),
        P(),
        P(),
        P(),
        P(),
        P(),
    )
    return jax.shard_map(
        local,
        mesh=mesh,
        in_specs=placed,
        out_specs=(P("gx", "gy", None), P(None, "gx", "gy", None)),
        check_vma=False,
    )
```

time: 118 us -> 111 us (0.941)
  blocking collectives: 30.8 us -> 73.7 us
  waiting for transfers between devices: 27.3 us -> 2.73 us
  starting transfers between devices: 37.4 us -> 19.8 us
  Pallas kernels: 16 us -> 10.4 us
  local copies, waits for them, and re-layouts: 4.22 us -> 2.45 us
    all_to_all x2 -> x0, waiting for transfers between devices: 23.7 us -> none  [the longest x1 12.2 us: local(): spread = lax.all_to_all(spread, 'gx', 0, 0, tiled=True)]
    all_to_all x1 -> x2, blocking collectives: 16.5 us -> 39.6 us  [local(): spread = lax.all_to_all(spread, 'gx', 0, 0, tiled=True)]
    all_to_all x0 -> x1, blocking collectives: none -> 19.7 us  [local(): sites = lax.all_to_all(sites, 'gy', 0, 0, tiled=True)]
    all_to_all x2 -> x0, starting transfers between devices: 16.3 us -> none  [the longest x1 10.8 us: local(): spread = lax.all_to_all(spread, 'gx', 0, 0, tiled=True)]
    ppermute x2, waiting for transfers between devices: 3.6 us -> 0.01 us  [the longest x1 0.01 us: local(): left = lax.ppermute(positions, 'gy', ring('gy', 1))]
    ppermute x1, waiting for transfers between devices: 0.01 us -> 2.72 us  [local(): before = lax.ppermute(column, 'gx', ring('gx', 1))]
    pallas_call x1, Pallas kernels: 5.1 us -> 2.86 us  [local(): pl.pallas_call(forward_kernel, name='forward', out_shape=shape(N_GX, 36,...]
    unnamed x45 -> x46, local copies, waits for them, and re-layouts: 3.24 us -> 1.46 us
  transfers between devices with their start and end apart: 6 -> 4, of which waited for: 3 -> 1; matrix products, arithmetic and copies ran while one was open for 2% -> 1% of each run, Pallas kernels for 0% -> 0%
where the time goes in v1:
time: 111 us
  blocking collectives  73.7 us (66%)
  starting transfers between devices  19.8 us (18%)
  Pallas kernels  10.4 us (9%)
  waiting for transfers between devices  2.73 us (2%)
  local copies, waits for them, and re-layouts  2.45 us (2%)
  between operations  1.58 us (1%)
    all_to_all x2, blocking collectives, local(): spread = lax.all_to_all(spread, 'gx', 0, 0, tiled=True)  39.6 us
    all_to_all x1, blocking collectives, local(): sites = lax.all_to_all(sites, 'gy', 0, 0, tiled=True)  19.7 us
    all_to_all x1, blocking collectives, local(): parts = lax.all_to_all(parts, 'gy', 0, 0, tiled=True)  14.3 us
    ppermute x1, starting transfers between devices, local(): right = lax.ppermute(positions, 'gy', ring('gy', -1))  9.5 us
    ppermute x1, starting transfers between devices, local(): left = lax.ppermute(positions, 'gy', ring('gy', 1))  4.38 us
    pallas_call x1, Pallas kernels, local(): pl.pallas_call(inverse_kernel, name='inverse', out_shape=shape(N_GY, 8, A...  3.28 us
    ppermute x1, starting transfers between devices, local(): before = lax.ppermute(column, 'gx', ring('gx', 1))  3.1 us
    pallas_call x1, Pallas kernels, local(): pl.pallas_call(forward_kernel, name='forward', out_shape=shape(N_GX, 36,...  2.86 us
  transfers between devices with their start and end apart: 4, of which 1 were waited for; matrix products, arithmetic and copies ran while one was open for 1% of the time, Pallas kernels for 0%

profile of v1, /device:TPU:1, one launch (start us, length us, event | category | flops | bytes accessed | tf_op | source)
XLA Modules:
  0.0 110.8 jit_solution(7971119854808696392)
XLA Ops:
  0.6 4.4 %collective-permute-start = (f32[3,1,1,128]{3,2,1,0:T(1,128)}, f32[3,1,1,128]{3,2,1,0:T(1,128)S(1)}, u32[]{:S(2)}, u32[]{:S(2)}) collective-permute-start(f32[3,1,1,128]{3,2,1,0:T(1,128)} %param.26), channel_id=1, source_target_pairs={{0,1},{1,2},{2,3},{3,4},{4,5},{5,6},{6,7},{7,8},{8,9},{9,10},{10,1... | collective-permute-start | bytes 4616 | tf_op jit(solution)/shard_map/ppermute | solution.py:453
  5.0 9.5 %collective-permute-start.1 = (f32[3,1,1,128]{3,2,1,0:T(1,128)}, f32[3,1,1,128]{3,2,1,0:T(1,128)S(1)}, u32[]{:S(2)}, u32[]{:S(2)}) collective-permute-start(f32[3,1,1,128]{3,2,1,0:T(1,128)} %param.26), channel_id=1, source_target_pairs={{0,15},{1,0},{2,1},{3,2},{4,3},{5,4},{6,5},{7,6},{8,7},{9,8},{10,9... | collective-permute-start | bytes 4616 | tf_op jit(solution)/shard_map/ppermute | solution.py:454
  14.6 0.7 dynamic-slice_bitcast_fusion
  15.2 0.1 broadcast_multiply_fusion.weight
  15.3 0.0 collective-permute-done
  15.3 0.7 copy-done.21
  16.0 0.0 collective-permute-done.1
  16.0 2.9 %collective-permute-start.3 = (f32[9,1,1,128]{3,2,1,0:T(1,128)S(1)}, f32[9,1,1,128]{3,2,1,0:T(1,128)S(1)}, u32[]{:S(2)}, u32[]{:S(2)}) collective-permute-start(f32[9,1,1,128]{3,2,1,0:T(1,128)S(1)} %constant_dynamic-update-slice_fusion.middle), channel_id=1, source_target_pairs={{0,496},{16,0},{32,16},{48,32},{64,48},{80,64},{96,80},{112,96},{1... | collective-permute-start | bytes 13832 | tf_op jit(solution)/shard_map/ppermute | solution.py:457
  18.9 3.1 %collective-permute-start.2 = (f32[9,1,1,128]{3,2,1,0:T(1,128)S(1)}, f32[9,1,1,128]{3,2,1,0:T(1,128)S(1)}, u32[]{:S(2)}, u32[]{:S(2)}) collective-permute-start(f32[9,1,1,128]{3,2,1,0:T(1,128)S(1)} %constant_dynamic-update-slice_fusion.middle), channel_id=1, source_target_pairs={{0,16},{16,32},{32,48},{48,64},{64,80},{80,96},{96,112},{112,128},... | collective-permute-start | bytes 13832 | tf_op jit(solution)/shard_map/ppermute | solution.py:456
  22.0 0.1 broadcast_add_fusion.square
  22.7 0.0 copy-done.20
  22.8 0.0 copy-start
  22.8 0.0 copy-start.11
  22.8 0.0 copy-start.12
  22.8 0.3 copy.27.gain
  23.1 0.0 collective-permute-done.3.after
  23.1 2.7 %collective-permute-done.2.before = f32[9,1,1,128]{3,2,1,0:T(1,128)S(1)} collective-permute-done((f32[9,1,1,128]{3,2,1,0:T(1,128)S(1)}, f32[9,1,1,128]{3,2,1,0:T(1,128)S(1)}, u32[]{:S(2)}, u32[]{:S(2)}) %collective-permute-start.2) | collective-permute-done | bytes 4640 | tf_op jit(solution)/shard_map/ppermute | solution.py:456
  25.8 0.0 copy-start.15
  25.9 0.0 copy-start.16
  25.9 0.0 copy-start.17
  25.9 0.0 copy-done
  25.9 0.0 copy-done.11
  25.9 0.0 copy-done.12
  25.9 0.6 copy-done.13
  26.5 0.0 copy-done.18
  26.5 0.0 copy-done.14
  26.6 0.0 copy-done.15
  26.6 0.0 copy-done.16
  26.6 0.0 copy-done.17
  26.6 1.9 %charge.1 = (f32[16,8,128]{2,1,0:T(8,128)S(1)}, f32[1,1,128]{2,1,0:T(1,128)S(1)}) custom-call(s32[1,1]{1,0:T(1,128)S(6)} %copy.30.count, f32[9,1,1,128]{3,2,1,0:T(1,128)S(1)} %collective-permute-done.2.before, f32[9,1,1,128]{3,2,1,0:T(1,128)S(1)} %constant_dynamic-update-slice_fusion.middle, f32[9,1,1,128]{3,2,1,0:T(1,128)S(1)} %collective-permute-done.3.after, ...), custom_call_target="tpu_custom_call" | custom-call | tf_op jit(solution)/shard_map/charge/pallas_call | solution.py:471
  28.5 19.7 %all_to_all.20.sites = f32[16,8,128]{2,1,0:T(8,128)S(1)} all-to-all(f32[16,8,128]{2,1,0:T(8,128)S(1)} %get-tuple-element.12), channel_id=1, replica_groups=mesh['gx'=32,'gy'=16] {'gy'}, dimensions={0} | all-to-all | bytes 131072 | tf_op jit(solution)/shard_map/all_to_all | solution.py:501
  48.3 0.0 copy-done.4
  48.3 2.9 %forward.1 = f32[32,36,128]{2,1,0:T(8,128)S(1)} custom-call(s32[1]{0:T(128)} %bitcast.device, f32[16,8,128]{2,1,0:T(8,128)S(1)} %all_to_all.20.sites, bf16[512,192]{1,0:T(8,128)(2,1)S(1)} %copy-done.4, bf16[512,192]{1,0:T(8,128)(2,1)S(1)} %copy-done.3), custom_call_target="tpu_custom_call" | custom-call | tf_op jit(solution)/shard_map/forward/pallas_call | solution.py:503
  51.1 0.0 copy-start.1
  51.1 0.0 copy-start.2
  51.2 0.0 copy-start.5
  51.2 0.0 copy-start.6
  51.2 0.0 copy-start.7
  51.2 0.0 copy-start.8
  51.2 23.1 %all_to_all.21.got = f32[32,36,128]{2,1,0:T(8,128)S(1)} all-to-all(f32[32,36,128]{2,1,0:T(8,128)S(1)} %forward.1), channel_id=1, replica_groups=mesh['gx'=32,'gy'=16] {'gx'}, dimensions={0} | all-to-all | bytes 1179648 | tf_op jit(solution)/shard_map/all_to_all | solution.py:517
  74.3 0.0 copy-done.1
  74.3 1.7 %convolve.1 = f32[32,36,128]{2,1,0:T(8,128)S(1)} custom-call(f32[3,128]{1,0:T(4,128)S(1)} %broadcast_add_fusion.square, f32[3,128]{1,0:T(4,128)S(1)} %broadcast_multiply_fusion.weight, f32[384,128]{1,0:T(8,128)S(1)} %copy-done.8, f32[384,128]{1,0:T(8,128)S(1)} %copy-done.7, bf16[384,256]{1,0:T(8,128)(2,1)S(1)} %copy-done.6, bf16[384,256]{1,0:T(8,128)(2,1)S(1)} %copy-done.5, ...), custom_call_target="tpu_custom_call" | custom-call | tf_op jit(solution)/shard_map/convolve/pallas_call | solution.py:519
  76.0 0.0 copy-start.9
  76.0 0.0 copy-start.10
  76.0 16.5 %all_to_all.22.got = f32[32,36,128]{2,1,0:T(8,128)S(1)} all-to-all(f32[32,36,128]{2,1,0:T(8,128)S(1)} %convolve.1), channel_id=1, replica_groups=mesh['gx'=32,'gy'=16] {'gx'}, dimensions={0} | all-to-all | bytes 1179648 | tf_op jit(solution)/shard_map/all_to_all | solution.py:528
  92.6 3.3 %inverse.1 = f32[16,8,128]{2,1,0:T(8,128)S(1)} custom-call(s32[1]{0:T(128)} %bitcast.device, f32[16,8,128]{2,1,0:T(8,128)S(1)} %all_to_all.20.sites, bf16[384,256]{1,0:T(8,128)(2,1)S(1)} %copy-done.10, bf16[384,256]{1,0:T(8,128)(2,1)S(1)} %copy-done.9, f32[32,36,128]{2,1,0:T(8,128)S(1)} %all_to_all.22.got), custom_call_target="tpu_custom_call" | custom-call | tf_op jit(solution)/shard_map/inverse/pallas_call | solution.py:530
  95.9 14.3 %all_to_all.23.parts = f32[16,8,128]{2,1,0:T(8,128)S(1)} all-to-all(f32[16,8,128]{2,1,0:T(8,128)S(1)} %inverse.1), channel_id=1, replica_groups=mesh['gx'=32,'gy'=16] {'gy'}, dimensions={0} | all-to-all | bytes 131072 | tf_op jit(solution)/shard_map/all_to_all | solution.py:545
  110.2 0.6 finish.1
  (22 shorter events, 0.1 us)
Async XLA Ops:
  0.6 14.7 %collective-permute-start = (f32[3,1,1,128]{3,2,1,0:T(1,128)}, f32[3,1,1,128]{3,2,1,0:T(1,128)S(1)}, u32[]{:S(2)}, u32[]{:S(2)}) collective-permute-start(f32[3,1,1,128]{3,2,1,0:T(1,128)} %param.26), channel_id=1, source_target_pairs={{0,1},{1,2},{2,3},{3,4},{4,5},{5,6},{6,7},{7,8},{8,9},{9,10},{10,1... | collective-permute-start | bytes 4616 | tf_op jit(solution)/shard_map/ppermute | solution.py:453
  5.0 11.0 %collective-permute-start.1 = (f32[3,1,1,128]{3,2,1,0:T(1,128)}, f32[3,1,1,128]{3,2,1,0:T(1,128)S(1)}, u32[]{:S(2)}, u32[]{:S(2)}) collective-permute-start(f32[3,1,1,128]{3,2,1,0:T(1,128)} %param.26), channel_id=1, source_target_pairs={{0,15},{1,0},{2,1},{3,2},{4,3},{5,4},{6,5},{7,6},{8,7},{9,8},{10,9... | collective-permute-start | bytes 4616 | tf_op jit(solution)/shard_map/ppermute | solution.py:454
  15.3 0.7 copy-start.21
  16.0 6.7 %copy-start.20 = (f32[1600]{0:T(1024)S(1)}, f32[1600]{0:T(1024)}, u32[]{:S(2)}) copy-start(f32[1600]{0:T(1024)} %param.33) | copy-start | bytes 19204
  16.0 7.1 %collective-permute-start.3 = (f32[9,1,1,128]{3,2,1,0:T(1,128)S(1)}, f32[9,1,1,128]{3,2,1,0:T(1,128)S(1)}, u32[]{:S(2)}, u32[]{:S(2)}) collective-permute-start(f32[9,1,1,128]{3,2,1,0:T(1,128)S(1)} %constant_dynamic-update-slice_fusion.middle), channel_id=1, source_target_pairs={{0,496},{16,0},{32,16},{48,32},{64,48},{80,64},{96,80},{112,96},{1... | collective-permute-start | bytes 13832 | tf_op jit(solution)/shard_map/ppermute | solution.py:457
  18.9 6.9 %collective-permute-start.2 = (f32[9,1,1,128]{3,2,1,0:T(1,128)S(1)}, f32[9,1,1,128]{3,2,1,0:T(1,128)S(1)}, u32[]{:S(2)}, u32[]{:S(2)}) collective-permute-start(f32[9,1,1,128]{3,2,1,0:T(1,128)S(1)} %constant_dynamic-update-slice_fusion.middle), channel_id=1, source_target_pairs={{0,16},{16,32},{32,48},{48,64},{64,80},{80,96},{96,112},{112,128},... | collective-permute-start | bytes 13832 | tf_op jit(solution)/shard_map/ppermute | solution.py:456
  22.8 3.1 %copy-start = (bf16[128,1600]{0,1:T(8,128)(2,1)S(1)}, bf16[128,1600]{0,1:T(8,128)(2,1)}, u32[]{:S(2)}) copy-start(bf16[128,1600]{0,1:T(8,128)(2,1)} %param.34) | copy-start | bytes 1228804
  22.8 3.1 %copy-start.11 = (bf16[128,128]{1,0:T(8,128)(2,1)S(1)}, bf16[128,128]{1,0:T(8,128)(2,1)}, u32[]{:S(2)}) copy-start(bf16[128,128]{1,0:T(8,128)(2,1)} %fit_hidden.1) | copy-start | bytes 98308
  22.8 3.1 %copy-start.12 = (s32[32,1,1,128]{3,2,1,0:T(1,128)S(1)}, s32[32,1,1,128]{3,2,1,0:T(1,128)}, u32[]{:S(2)}) copy-start(s32[32,1,1,128]{3,2,1,0:T(1,128)} %param.27) | copy-start | bytes 49156
  25.8 0.7 copy-start.13
  25.8 0.7 copy-start.18
  25.8 0.7 copy-start.19
  25.8 0.7 copy-start.14
  25.8 0.7 copy-start.15
  25.9 0.7 copy-start.16
  25.9 0.7 copy-start.17
  26.6 21.7 %copy-start.3 = (bf16[512,192]{1,0:T(8,128)(2,1)S(1)}, bf16[512,192]{1,0:T(8,128)(2,1)}, u32[]{:S(2)}) copy-start(bf16[512,192]{1,0:T(8,128)(2,1)} %constant.85.clone.odd) | copy-start | bytes 589828
  26.6 21.7 %copy-start.4 = (bf16[512,192]{1,0:T(8,128)(2,1)S(1)}, bf16[512,192]{1,0:T(8,128)(2,1)}, u32[]{:S(2)}) copy-start(bf16[512,192]{1,0:T(8,128)(2,1)} %constant.84.clone.even) | copy-start | bytes 589828
  51.1 23.1 %copy-start.1 = (bf16[512,192]{1,0:T(8,128)(2,1)S(1)}, bf16[512,192]{1,0:T(8,128)(2,1)}, u32[]{:S(2)}) copy-start(bf16[512,192]{1,0:T(8,128)(2,1)} %constant.91.clone.out_odd) | copy-start | bytes 589828
  51.1 23.1 %copy-start.2 = (bf16[512,192]{1,0:T(8,128)(2,1)S(1)}, bf16[512,192]{1,0:T(8,128)(2,1)}, u32[]{:S(2)}) copy-start(bf16[512,192]{1,0:T(8,128)(2,1)} %constant.90.clone.out_even) | copy-start | bytes 589828
  51.2 23.1 %copy-start.5 = (bf16[384,256]{1,0:T(8,128)(2,1)S(1)}, bf16[384,256]{1,0:T(8,128)(2,1)}, u32[]{:S(2)}) copy-start(bf16[384,256]{1,0:T(8,128)(2,1)} %constant.89.clone.in_odd) | copy-start | bytes 589828
  51.2 23.1 %copy-start.6 = (bf16[384,256]{1,0:T(8,128)(2,1)S(1)}, bf16[384,256]{1,0:T(8,128)(2,1)}, u32[]{:S(2)}) copy-start(bf16[384,256]{1,0:T(8,128)(2,1)} %constant.88.clone.in_even) | copy-start | bytes 589828
  51.2 23.1 %copy-start.7 = (f32[384,128]{1,0:T(8,128)S(1)}, f32[384,128]{1,0:T(8,128)}, u32[]{:S(2)}) copy-start(f32[384,128]{1,0:T(8,128)} %constant.87.clone.wx) | copy-start | bytes 589828
  51.2 23.1 %copy-start.8 = (f32[384,128]{1,0:T(8,128)S(1)}, f32[384,128]{1,0:T(8,128)}, u32[]{:S(2)}) copy-start(f32[384,128]{1,0:T(8,128)} %constant.86.clone.sx) | copy-start | bytes 589828
  76.0 16.6 %copy-start.9 = (bf16[384,256]{1,0:T(8,128)(2,1)S(1)}, bf16[384,256]{1,0:T(8,128)(2,1)}, u32[]{:S(2)}) copy-start(bf16[384,256]{1,0:T(8,128)(2,1)} %constant.93.clone.odd) | copy-start | bytes 589828
  76.0 16.6 %copy-start.10 = (bf16[384,256]{1,0:T(8,128)(2,1)S(1)}, bf16[384,256]{1,0:T(8,128)(2,1)}, u32[]{:S(2)}) copy-start(bf16[384,256]{1,0:T(8,128)(2,1)} %constant.92.clone.even) | copy-start | bytes 589828

commit v2 on v1

--- a/solution.py
+++ b/solution.py
@@ -105,7 +105,7 @@
 
 
 def charge_kernel(
-    count, before, middle, after, listed, base, weight, scale, bias, bias_one, bias_two, read_out,
+    count, parity, chip, middle, core, listed, base, weight, scale, bias, bias_one, bias_two, read_out,
     gain, fit_in, fit_hidden, sites, own, vectors, mixed, descriptor, normed,
 ):
     vectors[0:1, 0:EMB] = scale[...]
@@ -116,11 +116,17 @@
     block = lax.shift_right_logical(entry, 7)
     slot = jnp.bitwise_and(entry, ATOMS - 1)
     picked = [jnp.zeros((NEIGH, ATOMS), f32) for _ in range(3)]
-    for a, rows in enumerate((before, middle, after)):
+    is_even = jnp.full((1, ATOMS), parity[0], jnp.int32) == 0
+    rows_of = (
+        lambda r: jnp.where(is_even, chip[r, 0], core[r, 0]),
+        lambda r: middle[r, 0],
+        lambda r: jnp.where(is_even, core[r, 0], chip[r, 0]),
+    )
+    for a, rows in enumerate(rows_of):
         for b in range(3):
             here = block == a * 3 + b
             for c, shift in enumerate(((a - 1) * CX, (b - 1) * CY, 0)):
-                row = rows[b * 3 + c, 0] + float(shift)
+                row = rows(b * 3 + c) + float(shift)
                 row = jnp.broadcast_to(row, (NEIGH, ATOMS))
                 value = jnp.take_along_axis(row, slot, axis=1)
                 picked[c] = jnp.where(here, value, picked[c])
@@ -453,11 +459,13 @@
     left = lax.ppermute(positions, "gy", ring("gy", 1))
     right = lax.ppermute(positions, "gy", ring("gy", -1))
     column = jnp.concatenate([left, positions, right], axis=0)
-    before = lax.ppermute(column, "gx", ring("gx", 1))
-    after = lax.ppermute(column, "gx", ring("gx", -1))
+    pairs = range(N_GX)
+    across = [(i, (i + 1 if i % 2 else i - 1) % N_GX) for i in pairs]
+    chip = lax.ppermute(column, "gx", across)
+    core = lax.ppermute(column, "gx", [(i, i ^ 1) for i in pairs])
 
     gx, gy = lax.axis_index("gx"), lax.axis_index("gy")
-    device = gy.reshape(1)
+    device, parity = gy.reshape(1), (gx % 2).reshape(1)
     slot = (gx // 4) * 3 + jnp.arange(3)
     freq_z = gy * 12 + slot % 12
     square_z = jnp.square(freq_z.astype(f32) * WAVE)
@@ -465,14 +473,14 @@
     quarter = gx % 4
     square = square_z[:, None] + jnp.asarray(SQUARE_Y)[quarter]
     weight = weight_z[:, None] * jnp.asarray(WEIGHT_Y)[quarter]
-    middle, gain, device, square, weight = lax.optimization_barrier(
-        (column, desc_gain.reshape(DESC, 1), device, square, weight)
+    middle, gain, device, parity, square, weight = lax.optimization_barrier(
+        (column, desc_gain.reshape(DESC, 1), device, parity, square, weight)
     )
     sites, own = pl.pallas_call(
         charge_kernel,
         name="charge",
         out_shape=(shape(N_GY, 8, ATOMS), shape(1, 1, ATOMS)),
-        in_specs=[SMEM] + vmem(14),
+        in_specs=[SMEM, SMEM] + vmem(14),
         out_specs=tuple(vmem(2)),
         scratch_shapes=[
             pltpu.VMEM((8, ATOMS), f32),
@@ -483,9 +491,10 @@
         compiler_params=PARAMS,
     )(
         live_count,
-        before,
+        parity,
+        chip,
         middle,
-        after,
+        core,
         neighbours.reshape(NEIGH, ATOMS),
         stencil_base.reshape(3, 1, 1, ATOMS),
         spline_weight,

time: 111 us -> 110 us (level)
  waiting for transfers between devices: 2.73 us -> 0.71 us
    ppermute x2, waiting for transfers between devices: 2.72 us -> 0.7 us  [the longest x1 0.7 us: local(): chip = lax.ppermute(column, 'gx', across)]
where the time goes in v2:
time: 110 us
  blocking collectives  74.8 us (68%)
  starting transfers between devices  19.8 us (18%)
  Pallas kernels  10.3 us (9%)
  local copies, waits for them, and re-layouts  2.46 us (2%)
  between operations  1.6 us (1%)
    all_to_all x2, blocking collectives, local(): spread = lax.all_to_all(spread, 'gx', 0, 0, tiled=True)  39.6 us
    all_to_all x1, blocking collectives, local(): sites = lax.all_to_all(sites, 'gy', 0, 0, tiled=True)  20.8 us
    all_to_all x1, blocking collectives, local(): parts = lax.all_to_all(parts, 'gy', 0, 0, tiled=True)  14.3 us
    ppermute x1, starting transfers between devices, local(): right = lax.ppermute(positions, 'gy', ring('gy', -1))  9.5 us
    ppermute x1, starting transfers between devices, local(): left = lax.ppermute(positions, 'gy', ring('gy', 1))  4.38 us
    pallas_call x1, Pallas kernels, local(): pl.pallas_call(inverse_kernel, name='inverse', out_shape=shape(N_GY, 8, A...  3.28 us
    ppermute x1, starting transfers between devices, local(): chip = lax.ppermute(column, 'gx', across)  3.1 us
    pallas_call x1, Pallas kernels, local(): pl.pallas_call(forward_kernel, name='forward', out_shape=shape(N_GX, 36,...  2.87 us
  transfers between devices with their start and end apart: 4, of which 1 were waited for; matrix products, arithmetic and copies ran while one was open for 1% of the time, Pallas kernels for 0%

profile of v2, /device:TPU:1, one launch (start us, length us, event | category | flops | bytes accessed | tf_op | source)
XLA Modules:
  0.0 109.9 jit_solution(18438973654467956849)
XLA Ops:
  0.6 4.4 %collective-permute-start = (f32[3,1,1,128]{3,2,1,0:T(1,128)}, f32[3,1,1,128]{3,2,1,0:T(1,128)S(1)}, u32[]{:S(2)}, u32[]{:S(2)}) collective-permute-start(f32[3,1,1,128]{3,2,1,0:T(1,128)} %param.26), channel_id=1, source_target_pairs={{0,1},{1,2},{2,3},{3,4},{4,5},{5,6},{6,7},{7,8},{8,9},{9,10},{10,1... | collective-permute-start | bytes 4616 | tf_op jit(solution)/shard_map/ppermute | solution.py:459
  5.0 9.5 %collective-permute-start.1 = (f32[3,1,1,128]{3,2,1,0:T(1,128)}, f32[3,1,1,128]{3,2,1,0:T(1,128)S(1)}, u32[]{:S(2)}, u32[]{:S(2)}) collective-permute-start(f32[3,1,1,128]{3,2,1,0:T(1,128)} %param.26), channel_id=1, source_target_pairs={{0,15},{1,0},{2,1},{3,2},{4,3},{5,4},{6,5},{7,6},{8,7},{9,8},{10,9... | collective-permute-start | bytes 4616 | tf_op jit(solution)/shard_map/ppermute | solution.py:460
  14.6 0.7 dynamic-slice_bitcast_fusion
  15.3 0.1 broadcast_multiply_fusion.weight
  15.3 0.0 collective-permute-done
  15.3 0.7 copy-done.21
  16.0 0.0 collective-permute-done.1
  16.0 2.9 %collective-permute-start.3 = (f32[9,1,1,128]{3,2,1,0:T(1,128)S(1)}, f32[9,1,1,128]{3,2,1,0:T(1,128)S(1)}, u32[]{:S(2)}, u32[]{:S(2)}) collective-permute-start(f32[9,1,1,128]{3,2,1,0:T(1,128)S(1)} %constant_dynamic-update-slice_fusion.middle), channel_id=1, source_target_pairs={{0,16},{16,0},{32,48},{48,32},{64,80},{80,64},{96,112},{112,96},{1... | collective-permute-start | bytes 13832 | tf_op jit(solution)/shard_map/ppermute | solution.py:465
  18.9 3.1 %collective-permute-start.2 = (f32[9,1,1,128]{3,2,1,0:T(1,128)S(1)}, f32[9,1,1,128]{3,2,1,0:T(1,128)S(1)}, u32[]{:S(2)}, u32[]{:S(2)}) collective-permute-start(f32[9,1,1,128]{3,2,1,0:T(1,128)S(1)} %constant_dynamic-update-slice_fusion.middle), channel_id=1, source_target_pairs={{0,496},{16,32},{32,16},{48,64},{64,48},{80,96},{96,80},{112,128},... | collective-permute-start | bytes 13832 | tf_op jit(solution)/shard_map/ppermute | solution.py:464
  22.0 0.0 copy-start.20
  22.0 0.1 broadcast_add_fusion.square
  22.7 0.0 copy-done.20
  22.8 0.0 copy-start
  22.8 0.0 copy-start.11
  22.8 0.0 copy-start.12
  22.8 0.3 copy.27.gain
  23.1 0.0 collective-permute-done.3.core
  23.1 0.7 collective-permute-done.2.chip
  23.8 0.0 copy-start.15
  23.8 0.0 copy-start.16
  23.9 0.0 copy-start.17
  23.9 0.0 copy-done
  23.9 0.0 copy-done.11
  23.9 0.0 copy-done.12
  23.9 0.6 copy-done.13
  24.5 0.0 copy-done.18
  24.5 0.0 copy-done.14
  24.6 0.0 copy-done.16
  24.6 0.0 copy-done.17
  24.6 1.9 %charge.1 = (f32[16,8,128]{2,1,0:T(8,128)S(1)}, f32[1,1,128]{2,1,0:T(1,128)S(1)}) custom-call(s32[1,1]{1,0:T(1,128)S(6)} %copy.30.count, s32[1]{0:T(128)} %bitcast.1.parity, f32[9,1,1,128]{3,2,1,0:T(1,128)S(1)} %collective-permute-done.2.chip, f32[9,1,1,128]{3,2,1,0:T(1,128)S(1)} %constant_dynamic-update-slice_fusion.middle, ...), custom_call_target="tpu_custom_call" | custom-call | tf_op jit(solution)/shard_map/charge/pallas_call | solution.py:479
  26.5 20.8 %all_to_all.20.sites = f32[16,8,128]{2,1,0:T(8,128)S(1)} all-to-all(f32[16,8,128]{2,1,0:T(8,128)S(1)} %get-tuple-element.14), channel_id=1, replica_groups=mesh['gx'=32,'gy'=16] {'gy'}, dimensions={0} | all-to-all | bytes 131072 | tf_op jit(solution)/shard_map/all_to_all | solution.py:510
  47.3 2.9 %forward.1 = f32[32,36,128]{2,1,0:T(8,128)S(1)} custom-call(s32[1]{0:T(128)} %bitcast.device, f32[16,8,128]{2,1,0:T(8,128)S(1)} %all_to_all.20.sites, bf16[512,192]{1,0:T(8,128)(2,1)S(1)} %copy-done.4, bf16[512,192]{1,0:T(8,128)(2,1)S(1)} %copy-done.3), custom_call_target="tpu_custom_call" | custom-call | tf_op jit(solution)/shard_map/forward/pallas_call | solution.py:512
  50.2 0.0 copy-start.1
  50.2 0.0 copy-start.2
  50.2 0.0 copy-start.5
  50.2 0.0 copy-start.6
  50.3 0.0 copy-start.7
  50.3 0.0 copy-start.8
  50.3 23.0 %all_to_all.21.got = f32[32,36,128]{2,1,0:T(8,128)S(1)} all-to-all(f32[32,36,128]{2,1,0:T(8,128)S(1)} %forward.1), channel_id=1, replica_groups=mesh['gx'=32,'gy'=16] {'gx'}, dimensions={0} | all-to-all | bytes 1179648 | tf_op jit(solution)/shard_map/all_to_all | solution.py:526
  73.3 0.0 copy-done.1
  73.4 1.7 %convolve.1 = f32[32,36,128]{2,1,0:T(8,128)S(1)} custom-call(f32[3,128]{1,0:T(4,128)S(1)} %broadcast_add_fusion.square, f32[3,128]{1,0:T(4,128)S(1)} %broadcast_multiply_fusion.weight, f32[384,128]{1,0:T(8,128)S(1)} %copy-done.8, f32[384,128]{1,0:T(8,128)S(1)} %copy-done.7, bf16[384,256]{1,0:T(8,128)(2,1)S(1)} %copy-done.6, bf16[384,256]{1,0:T(8,128)(2,1)S(1)} %copy-done.5, ...), custom_call_target="tpu_custom_call" | custom-call | tf_op jit(solution)/shard_map/convolve/pallas_call | solution.py:528
  75.1 0.0 copy-start.9
  75.1 0.0 copy-start.10
  75.1 16.6 %all_to_all.22.got = f32[32,36,128]{2,1,0:T(8,128)S(1)} all-to-all(f32[32,36,128]{2,1,0:T(8,128)S(1)} %convolve.1), channel_id=1, replica_groups=mesh['gx'=32,'gy'=16] {'gx'}, dimensions={0} | all-to-all | bytes 1179648 | tf_op jit(solution)/shard_map/all_to_all | solution.py:537
  91.7 0.0 copy-done.10
  91.7 3.3 %inverse.1 = f32[16,8,128]{2,1,0:T(8,128)S(1)} custom-call(s32[1]{0:T(128)} %bitcast.device, f32[16,8,128]{2,1,0:T(8,128)S(1)} %all_to_all.20.sites, bf16[384,256]{1,0:T(8,128)(2,1)S(1)} %copy-done.10, bf16[384,256]{1,0:T(8,128)(2,1)S(1)} %copy-done.9, f32[32,36,128]{2,1,0:T(8,128)S(1)} %all_to_all.22.got), custom_call_target="tpu_custom_call" | custom-call | tf_op jit(solution)/shard_map/inverse/pallas_call | solution.py:539
  95.0 14.3 %all_to_all.23.parts = f32[16,8,128]{2,1,0:T(8,128)S(1)} all-to-all(f32[16,8,128]{2,1,0:T(8,128)S(1)} %inverse.1), channel_id=1, replica_groups=mesh['gx'=32,'gy'=16] {'gy'}, dimensions={0} | all-to-all | bytes 131072 | tf_op jit(solution)/shard_map/all_to_all | solution.py:554
  109.3 0.6 finish.1
  (22 shorter events, 0.1 us)
Async XLA Ops:
  0.6 14.7 %collective-permute-start = (f32[3,1,1,128]{3,2,1,0:T(1,128)}, f32[3,1,1,128]{3,2,1,0:T(1,128)S(1)}, u32[]{:S(2)}, u32[]{:S(2)}) collective-permute-start(f32[3,1,1,128]{3,2,1,0:T(1,128)} %param.26), channel_id=1, source_target_pairs={{0,1},{1,2},{2,3},{3,4},{4,5},{5,6},{6,7},{7,8},{8,9},{9,10},{10,1... | collective-permute-start | bytes 4616 | tf_op jit(solution)/shard_map/ppermute | solution.py:459
  5.0 11.0 %collective-permute-start.1 = (f32[3,1,1,128]{3,2,1,0:T(1,128)}, f32[3,1,1,128]{3,2,1,0:T(1,128)S(1)}, u32[]{:S(2)}, u32[]{:S(2)}) collective-permute-start(f32[3,1,1,128]{3,2,1,0:T(1,128)} %param.26), channel_id=1, source_target_pairs={{0,15},{1,0},{2,1},{3,2},{4,3},{5,4},{6,5},{7,6},{8,7},{9,8},{10,9... | collective-permute-start | bytes 4616 | tf_op jit(solution)/shard_map/ppermute | solution.py:460
  15.3 0.7 copy-start.21
  16.0 7.1 %collective-permute-start.3 = (f32[9,1,1,128]{3,2,1,0:T(1,128)S(1)}, f32[9,1,1,128]{3,2,1,0:T(1,128)S(1)}, u32[]{:S(2)}, u32[]{:S(2)}) collective-permute-start(f32[9,1,1,128]{3,2,1,0:T(1,128)S(1)} %constant_dynamic-update-slice_fusion.middle), channel_id=1, source_target_pairs={{0,16},{16,0},{32,48},{48,32},{64,80},{80,64},{96,112},{112,96},{1... | collective-permute-start | bytes 13832 | tf_op jit(solution)/shard_map/ppermute | solution.py:465
  18.9 4.9 %collective-permute-start.2 = (f32[9,1,1,128]{3,2,1,0:T(1,128)S(1)}, f32[9,1,1,128]{3,2,1,0:T(1,128)S(1)}, u32[]{:S(2)}, u32[]{:S(2)}) collective-permute-start(f32[9,1,1,128]{3,2,1,0:T(1,128)S(1)} %constant_dynamic-update-slice_fusion.middle), channel_id=1, source_target_pairs={{0,496},{16,32},{32,16},{48,64},{64,48},{80,96},{96,80},{112,128},... | collective-permute-start | bytes 13832 | tf_op jit(solution)/shard_map/ppermute | solution.py:464
  22.0 0.7 copy-start.20
  22.8 1.1 %copy-start = (bf16[128,1600]{0,1:T(8,128)(2,1)S(1)}, bf16[128,1600]{0,1:T(8,128)(2,1)}, u32[]{:S(2)}) copy-start(bf16[128,1600]{0,1:T(8,128)(2,1)} %param.34) | copy-start | bytes 1228804
  22.8 1.1 %copy-start.11 = (bf16[128,128]{1,0:T(8,128)(2,1)S(1)}, bf16[128,128]{1,0:T(8,128)(2,1)}, u32[]{:S(2)}) copy-start(bf16[128,128]{1,0:T(8,128)(2,1)} %fit_hidden.1) | copy-start | bytes 98308
  22.8 1.1 %copy-start.12 = (s32[32,1,1,128]{3,2,1,0:T(1,128)S(1)}, s32[32,1,1,128]{3,2,1,0:T(1,128)}, u32[]{:S(2)}) copy-start(s32[32,1,1,128]{3,2,1,0:T(1,128)} %param.27) | copy-start | bytes 49156
  23.8 0.7 copy-start.13
  23.8 0.7 copy-start.18
  23.8 0.7 copy-start.19
  23.8 0.7 copy-start.14
  23.8 0.7 copy-start.15
  23.8 0.7 copy-start.16
  23.9 0.7 copy-start.17
  24.6 22.8 %copy-start.3 = (bf16[512,192]{1,0:T(8,128)(2,1)S(1)}, bf16[512,192]{1,0:T(8,128)(2,1)}, u32[]{:S(2)}) copy-start(bf16[512,192]{1,0:T(8,128)(2,1)} %constant.93.clone.odd) | copy-start | bytes 589828
  24.6 22.8 %copy-start.4 = (bf16[512,192]{1,0:T(8,128)(2,1)S(1)}, bf16[512,192]{1,0:T(8,128)(2,1)}, u32[]{:S(2)}) copy-start(bf16[512,192]{1,0:T(8,128)(2,1)} %constant.92.clone.even) | copy-start | bytes 589828
  50.2 23.1 %copy-start.1 = (bf16[512,192]{1,0:T(8,128)(2,1)S(1)}, bf16[512,192]{1,0:T(8,128)(2,1)}, u32[]{:S(2)}) copy-start(bf16[512,192]{1,0:T(8,128)(2,1)} %constant.99.clone.out_odd) | copy-start | bytes 589828
  50.2 23.1 %copy-start.2 = (bf16[512,192]{1,0:T(8,128)(2,1)S(1)}, bf16[512,192]{1,0:T(8,128)(2,1)}, u32[]{:S(2)}) copy-start(bf16[512,192]{1,0:T(8,128)(2,1)} %constant.98.clone.out_even) | copy-start | bytes 589828
  50.2 23.1 %copy-start.5 = (bf16[384,256]{1,0:T(8,128)(2,1)S(1)}, bf16[384,256]{1,0:T(8,128)(2,1)}, u32[]{:S(2)}) copy-start(bf16[384,256]{1,0:T(8,128)(2,1)} %constant.97.clone.in_odd) | copy-start | bytes 589828
  50.2 23.1 %copy-start.6 = (bf16[384,256]{1,0:T(8,128)(2,1)S(1)}, bf16[384,256]{1,0:T(8,128)(2,1)}, u32[]{:S(2)}) copy-start(bf16[384,256]{1,0:T(8,128)(2,1)} %constant.96.clone.in_even) | copy-start | bytes 589828
  50.3 23.1 %copy-start.7 = (f32[384,128]{1,0:T(8,128)S(1)}, f32[384,128]{1,0:T(8,128)}, u32[]{:S(2)}) copy-start(f32[384,128]{1,0:T(8,128)} %constant.95.clone.wx) | copy-start | bytes 589828
  50.3 23.1 %copy-start.8 = (f32[384,128]{1,0:T(8,128)S(1)}, f32[384,128]{1,0:T(8,128)}, u32[]{:S(2)}) copy-start(f32[384,128]{1,0:T(8,128)} %constant.94.clone.sx) | copy-start | bytes 589828
  75.1 16.6 %copy-start.9 = (bf16[384,256]{1,0:T(8,128)(2,1)S(1)}, bf16[384,256]{1,0:T(8,128)(2,1)}, u32[]{:S(2)}) copy-start(bf16[384,256]{1,0:T(8,128)(2,1)} %constant.101.clone.odd) | copy-start | bytes 589828
  75.1 16.6 %copy-start.10 = (bf16[384,256]{1,0:T(8,128)(2,1)S(1)}, bf16[384,256]{1,0:T(8,128)(2,1)}, u32[]{:S(2)}) copy-start(bf16[384,256]{1,0:T(8,128)(2,1)} %constant.100.clone.even) | copy-start | bytes 589828

commit v3 on v2

--- a/solution.py
+++ b/solution.py
@@ -272,7 +272,7 @@
     return lax.broadcasted_iota(jnp.int32, (GRID, 128), 1) < WIN
 
 
-def forward_kernel(device, sites, even, odd, out, u_hi, u_lo, w, held):
+def forward_kernel(device, sites, even, odd, out, u, w, held):
     setup = z_setup(device[0])
     cells = []
     for pair in range(8):
@@ -287,12 +287,10 @@
             w[pair, WIN:, lanes] = lo
             (along_z,) = z_modes(setup, row(2), [spline(row(5))])
             for m in range(SLOTS):
-                hi, lo = split(along_z[m : m + 1, :] * table_x)
-                u_hi[pair, m * 16 : (m + 1) * 16, lanes] = hi
-                u_lo[pair, m * 16 : (m + 1) * 16, lanes] = lo
+                spread = along_z[m : m + 1, :] * table_x
+                u[pair, m * 16 : (m + 1) * 16, lanes] = spread.astype(bf16)
         dims = (((1,), (1,)), ((), ()))
-        both = lax.dot_general(u_hi[pair], w[pair], dims, preferred_element_type=f32)
-        both = both + lax.dot_general(u_lo[pair], w[pair], dims, preferred_element_type=f32)
+        both = lax.dot_general(u[pair], w[pair], dims, preferred_element_type=f32)
         cells.append(both + pltpu.roll(both, WIN, 1))
     front = first_half()
     tiles = [jnp.where(front, cells[2 * t], cells[2 * t + 1]) for t in range(4)]
@@ -517,7 +515,6 @@
         out_specs=vmem(1)[0],
         scratch_shapes=[
             pltpu.VMEM((8, GRID, PAIR), bf16),
-            pltpu.VMEM((8, GRID, PAIR), bf16),
             pltpu.VMEM((8, 2 * WIN, PAIR), bf16),
             pltpu.VMEM((GRID, SIDE), f32),
         ],

time: 110 us -> 110 us (level)
  no operation moved by 1% of the time
where the time goes in v3:
time: 110 us; the launch traced here: 109 us
  blocking collectives  74.8 us (68%)
  starting transfers between devices  19.8 us (18%)
  Pallas kernels  9.76 us (9%)
  local copies, waits for them, and re-layouts  2.46 us (2%)
  between operations  1.6 us (1%)
    all_to_all x2, blocking collectives, local(): spread = lax.all_to_all(spread, 'gx', 0, 0, tiled=True)  39.6 us
    all_to_all x1, blocking collectives, local(): sites = lax.all_to_all(sites, 'gy', 0, 0, tiled=True)  20.8 us
    all_to_all x1, blocking collectives, local(): parts = lax.all_to_all(parts, 'gy', 0, 0, tiled=True)  14.3 us
    ppermute x1, starting transfers between devices, local(): right = lax.ppermute(positions, 'gy', ring('gy', -1))  9.5 us
    ppermute x1, starting transfers between devices, local(): left = lax.ppermute(positions, 'gy', ring('gy', 1))  4.38 us
    pallas_call x1, Pallas kernels, local(): pl.pallas_call(inverse_kernel, name='inverse', out_shape=shape(N_GY, 8, A...  3.28 us
    ppermute x1, starting transfers between devices, local(): chip = lax.ppermute(column, 'gx', across)  3.1 us
    ppermute x1, starting transfers between devices, local(): core = lax.ppermute(column, 'gx', [(i, i ^ 1) for i in pairs])  2.86 us
  transfers between devices with their start and end apart: 4, of which 1 were waited for; matrix products, arithmetic and copies ran while one was open for 1% of the time, Pallas kernels for 0%

profile of v3, /device:TPU:1, one launch (start us, length us, event | category | flops | bytes accessed | tf_op | source)
XLA Modules:
  0.0 109.3 jit_solution(2000796739943512305)
XLA Ops:
  0.6 4.4 %collective-permute-start = (f32[3,1,1,128]{3,2,1,0:T(1,128)}, f32[3,1,1,128]{3,2,1,0:T(1,128)S(1)}, u32[]{:S(2)}, u32[]{:S(2)}) collective-permute-start(f32[3,1,1,128]{3,2,1,0:T(1,128)} %param.26), channel_id=1, source_target_pairs={{0,1},{1,2},{2,3},{3,4},{4,5},{5,6},{6,7},{7,8},{8,9},{9,10},{10,1... | collective-permute-start | bytes 4616 | tf_op jit(solution)/shard_map/ppermute | solution.py:457
  5.0 9.5 %collective-permute-start.1 = (f32[3,1,1,128]{3,2,1,0:T(1,128)}, f32[3,1,1,128]{3,2,1,0:T(1,128)S(1)}, u32[]{:S(2)}, u32[]{:S(2)}) collective-permute-start(f32[3,1,1,128]{3,2,1,0:T(1,128)} %param.26), channel_id=1, source_target_pairs={{0,15},{1,0},{2,1},{3,2},{4,3},{5,4},{6,5},{7,6},{8,7},{9,8},{10,9... | collective-permute-start | bytes 4616 | tf_op jit(solution)/shard_map/ppermute | solution.py:458
  14.6 0.7 dynamic-slice_bitcast_fusion
  15.3 0.1 broadcast_multiply_fusion.weight
  15.3 0.0 collective-permute-done
  15.3 0.7 copy-done.21
  16.0 0.0 collective-permute-done.1
  16.0 2.9 %collective-permute-start.3 = (f32[9,1,1,128]{3,2,1,0:T(1,128)S(1)}, f32[9,1,1,128]{3,2,1,0:T(1,128)S(1)}, u32[]{:S(2)}, u32[]{:S(2)}) collective-permute-start(f32[9,1,1,128]{3,2,1,0:T(1,128)S(1)} %constant_dynamic-update-slice_fusion.middle), channel_id=1, source_target_pairs={{0,16},{16,0},{32,48},{48,32},{64,80},{80,64},{96,112},{112,96},{1... | collective-permute-start | bytes 13832 | tf_op jit(solution)/shard_map/ppermute | solution.py:463
  18.9 3.1 %collective-permute-start.2 = (f32[9,1,1,128]{3,2,1,0:T(1,128)S(1)}, f32[9,1,1,128]{3,2,1,0:T(1,128)S(1)}, u32[]{:S(2)}, u32[]{:S(2)}) collective-permute-start(f32[9,1,1,128]{3,2,1,0:T(1,128)S(1)} %constant_dynamic-update-slice_fusion.middle), channel_id=1, source_target_pairs={{0,496},{16,32},{32,16},{48,64},{64,48},{80,96},{96,80},{112,128},... | collective-permute-start | bytes 13832 | tf_op jit(solution)/shard_map/ppermute | solution.py:462
  22.0 0.0 copy-start.20
  22.0 0.1 broadcast_add_fusion.square
  22.7 0.0 copy-done.20
  22.8 0.0 copy-start
  22.8 0.0 copy-start.11
  22.8 0.0 copy-start.12
  22.8 0.3 copy.27.gain
  23.1 0.0 collective-permute-done.3.core
  23.1 0.7 collective-permute-done.2.chip
  23.8 0.0 copy-start.15
  23.8 0.0 copy-start.16
  23.9 0.0 copy-start.17
  23.9 0.0 copy-done
  23.9 0.0 copy-done.11
  23.9 0.0 copy-done.12
  23.9 0.6 copy-done.13
  24.5 0.0 copy-done.14
  24.6 0.0 copy-done.16
  24.6 0.0 copy-done.17
  24.6 1.9 %charge.1 = (f32[16,8,128]{2,1,0:T(8,128)S(1)}, f32[1,1,128]{2,1,0:T(1,128)S(1)}) custom-call(s32[1,1]{1,0:T(1,128)S(6)} %copy.30.count, s32[1]{0:T(128)} %bitcast.1.parity, f32[9,1,1,128]{3,2,1,0:T(1,128)S(1)} %collective-permute-done.2.chip, f32[9,1,1,128]{3,2,1,0:T(1,128)S(1)} %constant_dynamic-update-slice_fusion.middle, ...), custom_call_target="tpu_custom_call" | custom-call | tf_op jit(solution)/shard_map/charge/pallas_call | solution.py:477
  26.5 20.8 %all_to_all.20.sites = f32[16,8,128]{2,1,0:T(8,128)S(1)} all-to-all(f32[16,8,128]{2,1,0:T(8,128)S(1)} %get-tuple-element.14), channel_id=1, replica_groups=mesh['gx'=32,'gy'=16] {'gy'}, dimensions={0} | all-to-all | bytes 131072 | tf_op jit(solution)/shard_map/all_to_all | solution.py:508
  47.3 0.0 copy-done.3
  47.3 2.3 %forward.1 = f32[32,36,128]{2,1,0:T(8,128)S(1)} custom-call(s32[1]{0:T(128)} %bitcast.device, f32[16,8,128]{2,1,0:T(8,128)S(1)} %all_to_all.20.sites, bf16[512,192]{1,0:T(8,128)(2,1)S(1)} %copy-done.4, bf16[512,192]{1,0:T(8,128)(2,1)S(1)} %copy-done.3), custom_call_target="tpu_custom_call" | custom-call | tf_op jit(solution)/shard_map/forward/pallas_call | solution.py:510
  49.6 0.0 copy-start.1
  49.6 0.0 copy-start.2
  49.6 0.0 copy-start.5
  49.7 0.0 copy-start.6
  49.7 0.0 copy-start.7
  49.7 0.0 copy-start.8
  49.7 23.0 %all_to_all.21.got = f32[32,36,128]{2,1,0:T(8,128)S(1)} all-to-all(f32[32,36,128]{2,1,0:T(8,128)S(1)} %forward.1), channel_id=1, replica_groups=mesh['gx'=32,'gy'=16] {'gx'}, dimensions={0} | all-to-all | bytes 1179648 | tf_op jit(solution)/shard_map/all_to_all | solution.py:523
  72.7 0.0 copy-done.2
  72.8 1.7 %convolve.1 = f32[32,36,128]{2,1,0:T(8,128)S(1)} custom-call(f32[3,128]{1,0:T(4,128)S(1)} %broadcast_add_fusion.square, f32[3,128]{1,0:T(4,128)S(1)} %broadcast_multiply_fusion.weight, f32[384,128]{1,0:T(8,128)S(1)} %copy-done.8, f32[384,128]{1,0:T(8,128)S(1)} %copy-done.7, bf16[384,256]{1,0:T(8,128)(2,1)S(1)} %copy-done.6, bf16[384,256]{1,0:T(8,128)(2,1)S(1)} %copy-done.5, ...), custom_call_target="tpu_custom_call" | custom-call | tf_op jit(solution)/shard_map/convolve/pallas_call | solution.py:525
  74.5 0.0 copy-start.9
  74.5 0.0 copy-start.10
  74.5 16.6 %all_to_all.22.got = f32[32,36,128]{2,1,0:T(8,128)S(1)} all-to-all(f32[32,36,128]{2,1,0:T(8,128)S(1)} %convolve.1), channel_id=1, replica_groups=mesh['gx'=32,'gy'=16] {'gx'}, dimensions={0} | all-to-all | bytes 1179648 | tf_op jit(solution)/shard_map/all_to_all | solution.py:534
  91.1 0.0 copy-done.9
  91.1 3.3 %inverse.1 = f32[16,8,128]{2,1,0:T(8,128)S(1)} custom-call(s32[1]{0:T(128)} %bitcast.device, f32[16,8,128]{2,1,0:T(8,128)S(1)} %all_to_all.20.sites, bf16[384,256]{1,0:T(8,128)(2,1)S(1)} %copy-done.10, bf16[384,256]{1,0:T(8,128)(2,1)S(1)} %copy-done.9, f32[32,36,128]{2,1,0:T(8,128)S(1)} %all_to_all.22.got), custom_call_target="tpu_custom_call" | custom-call | tf_op jit(solution)/shard_map/inverse/pallas_call | solution.py:536
  94.4 14.3 %all_to_all.23.parts = f32[16,8,128]{2,1,0:T(8,128)S(1)} all-to-all(f32[16,8,128]{2,1,0:T(8,128)S(1)} %inverse.1), channel_id=1, replica_groups=mesh['gx'=32,'gy'=16] {'gy'}, dimensions={0} | all-to-all | bytes 131072 | tf_op jit(solution)/shard_map/all_to_all | solution.py:551
  108.7 0.6 finish.1
  (22 shorter events, 0.1 us)
Async XLA Ops:
  0.6 14.7 %collective-permute-start = (f32[3,1,1,128]{3,2,1,0:T(1,128)}, f32[3,1,1,128]{3,2,1,0:T(1,128)S(1)}, u32[]{:S(2)}, u32[]{:S(2)}) collective-permute-start(f32[3,1,1,128]{3,2,1,0:T(1,128)} %param.26), channel_id=1, source_target_pairs={{0,1},{1,2},{2,3},{3,4},{4,5},{5,6},{6,7},{7,8},{8,9},{9,10},{10,1... | collective-permute-start | bytes 4616 | tf_op jit(solution)/shard_map/ppermute | solution.py:457
  5.0 11.0 %collective-permute-start.1 = (f32[3,1,1,128]{3,2,1,0:T(1,128)}, f32[3,1,1,128]{3,2,1,0:T(1,128)S(1)}, u32[]{:S(2)}, u32[]{:S(2)}) collective-permute-start(f32[3,1,1,128]{3,2,1,0:T(1,128)} %param.26), channel_id=1, source_target_pairs={{0,15},{1,0},{2,1},{3,2},{4,3},{5,4},{6,5},{7,6},{8,7},{9,8},{10,9... | collective-permute-start | bytes 4616 | tf_op jit(solution)/shard_map/ppermute | solution.py:458
  15.3 0.7 copy-start.21
  16.0 7.1 %collective-permute-start.3 = (f32[9,1,1,128]{3,2,1,0:T(1,128)S(1)}, f32[9,1,1,128]{3,2,1,0:T(1,128)S(1)}, u32[]{:S(2)}, u32[]{:S(2)}) collective-permute-start(f32[9,1,1,128]{3,2,1,0:T(1,128)S(1)} %constant_dynamic-update-slice_fusion.middle), channel_id=1, source_target_pairs={{0,16},{16,0},{32,48},{48,32},{64,80},{80,64},{96,112},{112,96},{1... | collective-permute-start | bytes 13832 | tf_op jit(solution)/shard_map/ppermute | solution.py:463
  18.9 4.9 %collective-permute-start.2 = (f32[9,1,1,128]{3,2,1,0:T(1,128)S(1)}, f32[9,1,1,128]{3,2,1,0:T(1,128)S(1)}, u32[]{:S(2)}, u32[]{:S(2)}) collective-permute-start(f32[9,1,1,128]{3,2,1,0:T(1,128)S(1)} %constant_dynamic-update-slice_fusion.middle), channel_id=1, source_target_pairs={{0,496},{16,32},{32,16},{48,64},{64,48},{80,96},{96,80},{112,128},... | collective-permute-start | bytes 13832 | tf_op jit(solution)/shard_map/ppermute | solution.py:462
  22.0 0.7 copy-start.20
  22.8 1.1 %copy-start = (bf16[128,1600]{0,1:T(8,128)(2,1)S(1)}, bf16[128,1600]{0,1:T(8,128)(2,1)}, u32[]{:S(2)}) copy-start(bf16[128,1600]{0,1:T(8,128)(2,1)} %param.34) | copy-start | bytes 1228804
  22.8 1.1 %copy-start.11 = (bf16[128,128]{1,0:T(8,128)(2,1)S(1)}, bf16[128,128]{1,0:T(8,128)(2,1)}, u32[]{:S(2)}) copy-start(bf16[128,128]{1,0:T(8,128)(2,1)} %fit_hidden.1) | copy-start | bytes 98308
  22.8 1.1 %copy-start.12 = (s32[32,1,1,128]{3,2,1,0:T(1,128)S(1)}, s32[32,1,1,128]{3,2,1,0:T(1,128)}, u32[]{:S(2)}) copy-start(s32[32,1,1,128]{3,2,1,0:T(1,128)} %param.27) | copy-start | bytes 49156
  23.8 0.7 copy-start.13
  23.8 0.7 copy-start.18
  23.8 0.7 copy-start.19
  23.8 0.7 copy-start.14
  23.8 0.7 copy-start.15
  23.8 0.7 copy-start.16
  23.9 0.7 copy-start.17
  24.6 22.8 %copy-start.3 = (bf16[512,192]{1,0:T(8,128)(2,1)S(1)}, bf16[512,192]{1,0:T(8,128)(2,1)}, u32[]{:S(2)}) copy-start(bf16[512,192]{1,0:T(8,128)(2,1)} %constant.93.clone.odd) | copy-start | bytes 589828
  24.6 22.8 %copy-start.4 = (bf16[512,192]{1,0:T(8,128)(2,1)S(1)}, bf16[512,192]{1,0:T(8,128)(2,1)}, u32[]{:S(2)}) copy-start(bf16[512,192]{1,0:T(8,128)(2,1)} %constant.92.clone.even) | copy-start | bytes 589828
  49.6 23.1 %copy-start.1 = (bf16[512,192]{1,0:T(8,128)(2,1)S(1)}, bf16[512,192]{1,0:T(8,128)(2,1)}, u32[]{:S(2)}) copy-start(bf16[512,192]{1,0:T(8,128)(2,1)} %constant.99.clone.out_odd) | copy-start | bytes 589828
  49.6 23.1 %copy-start.2 = (bf16[512,192]{1,0:T(8,128)(2,1)S(1)}, bf16[512,192]{1,0:T(8,128)(2,1)}, u32[]{:S(2)}) copy-start(bf16[512,192]{1,0:T(8,128)(2,1)} %constant.98.clone.out_even) | copy-start | bytes 589828
  49.6 23.1 %copy-start.5 = (bf16[384,256]{1,0:T(8,128)(2,1)S(1)}, bf16[384,256]{1,0:T(8,128)(2,1)}, u32[]{:S(2)}) copy-start(bf16[384,256]{1,0:T(8,128)(2,1)} %constant.97.clone.in_odd) | copy-start | bytes 589828
  49.7 23.1 %copy-start.6 = (bf16[384,256]{1,0:T(8,128)(2,1)S(1)}, bf16[384,256]{1,0:T(8,128)(2,1)}, u32[]{:S(2)}) copy-start(bf16[384,256]{1,0:T(8,128)(2,1)} %constant.96.clone.in_even) | copy-start | bytes 589828
  49.7 23.1 %copy-start.7 = (f32[384,128]{1,0:T(8,128)S(1)}, f32[384,128]{1,0:T(8,128)}, u32[]{:S(2)}) copy-start(f32[384,128]{1,0:T(8,128)} %constant.95.clone.wx) | copy-start | bytes 589828
  49.7 23.1 %copy-start.8 = (f32[384,128]{1,0:T(8,128)S(1)}, f32[384,128]{1,0:T(8,128)}, u32[]{:S(2)}) copy-start(f32[384,128]{1,0:T(8,128)} %constant.94.clone.sx) | copy-start | bytes 589828
  74.5 16.6 %copy-start.9 = (bf16[384,256]{1,0:T(8,128)(2,1)S(1)}, bf16[384,256]{1,0:T(8,128)(2,1)}, u32[]{:S(2)}) copy-start(bf16[384,256]{1,0:T(8,128)(2,1)} %constant.101.clone.odd) | copy-start | bytes 589828
  74.5 16.6 %copy-start.10 = (bf16[384,256]{1,0:T(8,128)(2,1)S(1)}, bf16[384,256]{1,0:T(8,128)(2,1)}, u32[]{:S(2)}) copy-start(bf16[384,256]{1,0:T(8,128)(2,1)} %constant.100.clone.even) | copy-start | bytes 589828
